TPU v7x, 512 devices: a whole 4x4x16 slice. The times are simulated.
512 devices in a mesh: seq: 32 (over z, core), batch: 4 (over y), state: 4 (over x).
Axes of the slice: x: 4, y: 4, z: 16, core: 2. Of those that a mesh axis runs over, the one named last changes fastest.
Arguments:
- inputs: bfloat16 [4, 8192, 2048], P('batch', 'seq', 'state'), may hold values from -6 to 6
- cotangent: bfloat16 [4, 8192, 2048], P('batch', 'seq', 'state'), may hold values from -0.125 to 0.125
- step_size: float32 [4, 8192], P('batch', 'seq'), may hold values from 0.35 to 18022.4, as said below
- resets: int32 [4, 8192], P('batch', 'seq'), may hold values 0 or 1
- log_decay: float32 [2, 512], P(None, 'state'), may hold values from -0.3 to 0.3, as said below
- in_proj: bfloat16 [2, 2048, 512], P(None, None, 'state'), may hold values from -0.125 to 0.125
- out_proj: bfloat16 [2, 2048, 512], P(None, None, 'state'), may hold values from -0.1875 to 0.1875
- saved_states: float32 [4, 128, 2, 512], P('batch', 'seq', None, 'state'), may hold values from -48 to 48
- saved_index: int32 [4, 128], P('batch', 'seq'), may hold values from 0 to 3, as said below
Outputs:
- grad_inputs: bfloat16 [4, 8192, 2048], P('batch', 'seq', 'state')
- grad_in_proj: float32 [2, 2048, 512], P(None, 'batch', 'state')
- grad_decay: float32 [2, 512], P(None, 'state')
Inputs may be any that keep to these rules, and one draw needn't show every extreme that they name: `step_size`: positive. `log_decay`: row 0 is negative. `saved_index`: within each aligned group of 4 spans, the values are a permutation of 0 to 3.
All inputs are finite; a program needn't handle non-finite values. No bound on the sum of `resets` on one device may be relied on, other than what follows from the above.
Results may differ from a plain program's by a relative error of at most 0.0049.
Values may be sent and summed in bfloat16 or wider, within the bound.
A program may use at most 64 MiB of HBM per device.

v0:
```python
import math

import jax
import jax.numpy as jnp
from jax import lax
from jax.sharding import PartitionSpec as P


def prefix(value, axis, join, neutral):
    count, mine = (lax.axis_size(axis), lax.axis_index(axis))
    pieces = jax.tree.map(lambda part: lax.all_gather(part, axis), value)
    pieces = jax.tree.map(lambda part: part[::-1], pieces)
    mine = count - 1 - mine
    so_far = jax.tree.map(
        lambda part, zero: jnp.full_like(part, 0) + jnp.asarray(zero, part.dtype), value, neutral
    )

    def turn(position, so_far):
        longer = join(so_far, jax.tree.map(lambda part: part[position], pieces))
        return jax.tree.map(lambda new, old: jnp.where(position < mine, new, old), longer, so_far)

    return lax.fori_loop(0, count - 1, turn, so_far)


def complex_times(left_re, left_im, right_re, right_im):
    return (left_re * right_re - left_im * right_im, left_re * right_im + left_im * right_re)


def forward_combine(earlier, later):
    early_ar, early_ai, early_br, early_bi = earlier
    late_ar, late_ai, late_br, late_bi = later
    prod_re, prod_im = complex_times(late_ar, late_ai, early_ar, early_ai)
    move_re, move_im = complex_times(late_ar, late_ai, early_br, early_bi)
    return (prod_re, prod_im, move_re + late_br, move_im + late_bi)


def backward_combine(after, current):
    after_pr, after_pi, after_gr, after_gi = after
    cur_cr, cur_ci, cur_er, cur_ei = current
    prod_re, prod_im = complex_times(cur_cr, cur_ci, after_pr, after_pi)
    move_re, move_im = complex_times(cur_cr, cur_ci, after_gr, after_gi)
    return (prod_re, prod_im, cur_er + move_re, cur_ei + move_im)


def decay_parts(step_size, resets, log_decay):
    keeping = (1 - resets).astype(jnp.float32)[..., None]
    scaled = step_size[..., None]
    magnitude = keeping * jnp.exp(scaled * log_decay[0])
    angle = scaled * log_decay[1]
    return (magnitude * jnp.cos(angle), magnitude * jnp.sin(angle))


def local(
    inputs, cotangent, step_size, resets, log_decay, in_proj, out_proj, saved_states, saved_index
):
    whole_in, whole_cot = (
        lax.all_gather(inputs, "state", axis=2, tiled=True),
        lax.all_gather(cotangent, "state", axis=2, tiled=True),
    )
    tok_in = whole_in[0]
    tok_cot = whole_cot[0]
    steps = tok_in.shape[0]
    states = in_proj.shape[2]
    decay_re, decay_im = decay_parts(step_size[0], resets[0], log_decay)
    drive = jnp.einsum("th,khp->ktp", tok_in, in_proj, preferred_element_type=jnp.float32)
    inject = jnp.einsum("th,khp->ktp", tok_cot, out_proj, preferred_element_type=jnp.float32)
    inject_re = inject[0]
    inject_im = -inject[1]
    slot_ids = saved_index[0]
    spans = slot_ids.shape[0]
    span_steps = steps // spans
    matches = slot_ids[:, None] == jnp.arange(spans, dtype=jnp.int32)[None, :]
    start_pair = jnp.sum(jnp.where(matches[:, :, None, None], saved_states[0][None], 0.0), axis=1)
    start_re = start_pair[:, 0][:, None, :]
    start_im = start_pair[:, 1][:, None, :]
    blocked = (spans, span_steps, states)
    elements = (
        decay_re.reshape(blocked),
        decay_im.reshape(blocked),
        drive[0].reshape(blocked),
        drive[1].reshape(blocked),
    )
    prod_re, prod_im, acc_re, acc_im = lax.associative_scan(forward_combine, elements, axis=1)
    carried_re, carried_im = complex_times(prod_re, prod_im, start_re, start_im)
    state_re = carried_re + acc_re
    state_im = carried_im + acc_im
    prior_re = jnp.concatenate([start_re, state_re[:, :-1]], axis=1).reshape(steps, states)
    prior_im = jnp.concatenate([start_im, state_im[:, :-1]], axis=1).reshape(steps, states)
    one_row = jnp.ones((1, states), jnp.float32)
    zero_row = jnp.zeros((1, states), jnp.float32)
    next_re = jnp.concatenate([decay_re[1:], one_row], axis=0)
    next_im = jnp.concatenate([-decay_im[1:], zero_row], axis=0)
    suffix_re, suffix_im, local_re, local_im = lax.associative_scan(
        backward_combine, (next_re, next_im, inject_re, inject_im), reverse=True, axis=0
    )
    total_re, total_im = complex_times(decay_re[0], -decay_im[0], suffix_re[0], suffix_im[0])
    summary_re, summary_im = complex_times(decay_re[0], -decay_im[0], local_re[0], local_im[0])
    zero_state = jnp.zeros((states,), jnp.float32)
    scanned = prefix(
        (total_re, total_im, summary_re, summary_im),
        "seq",
        backward_combine,
        (jnp.ones((states,), jnp.float32), zero_state, zero_state, zero_state),
    )
    incoming_re = scanned[2]
    incoming_im = scanned[3]
    reach_re, reach_im = complex_times(suffix_re, suffix_im, incoming_re[None], incoming_im[None])
    adjoint_re = local_re + reach_re
    adjoint_im = local_im + reach_im
    adjoint_bf = jnp.stack([adjoint_re, adjoint_im]).astype(jnp.bfloat16)
    grad_rows = lax.psum_scatter(
        jnp.einsum("khp,ktp->ht", in_proj, adjoint_bf, preferred_element_type=jnp.float32),
        "state",
        scatter_dimension=0,
        tiled=True,
    )
    grad_inputs = grad_rows.astype(jnp.bfloat16).T[None]
    partial_proj = jnp.einsum("th,ktp->khp", tok_in, adjoint_bf, preferred_element_type=jnp.float32)
    left_re, left_im = complex_times(decay_re, -decay_im, adjoint_re, adjoint_im)
    wide_re, wide_im = complex_times(left_re, left_im, prior_re, -prior_im)
    weight = step_size[0][:, None]
    partial_decay = jnp.stack(
        [jnp.sum(weight * wide_re, axis=0), jnp.sum(weight * wide_im, axis=0)]
    )
    batch_total = inputs.shape[0] * lax.axis_size("batch")
    length_total = steps * lax.axis_size("seq")
    row_scale = 1.0 / math.sqrt(batch_total * length_total)
    rows_batch = in_proj.shape[1] // lax.axis_size("batch")
    summed_proj, decay_total = lax.psum((partial_proj, partial_decay), ("seq", "batch"))
    own_rows = lax.dynamic_slice_in_dim(
        summed_proj, lax.axis_index("batch") * rows_batch, rows_batch, 1
    )
    grad_in_proj = own_rows * row_scale
    grad_decay = decay_total / (batch_total * length_total)
    return (grad_inputs, grad_in_proj, grad_decay)


def solution(mesh):
    in_specs = (
        P("batch", "seq", "state"),
        P("batch", "seq", "state"),
        P("batch", "seq"),
        P("batch", "seq"),
        P(None, "state"),
        P(None, None, "state"),
        P(None, None, "state"),
        P("batch", "seq", None, "state"),
        P("batch", "seq"),
    )
    out_specs = (P("batch", "seq", "state"), P(None, "batch", "state"), P(None, "state"))
    return jax.shard_map(local, mesh=mesh, in_specs=in_specs, out_specs=out_specs, check_vma=False)
```

profile of v0, /device:TPU:1, one launch (start us, length us, event | category | flops | bytes accessed | tf_op | source)
XLA Modules:
  0.0 748.4 jit_solution(6888337707852878612)
XLA Ops:
  11.6 2.2 slice.915
  13.8 2.2 slice.927
  16.1 2.2 slice.920
  18.4 2.2 slice.929
  20.6 2.2 slice.1032
  22.8 2.2 slice.911
  33.1 13.1 %all-gather.7.cloned.1.call-done = bf16[1,256,2048]{2,1,0:T(8,128)(2,1)} async-done(((bf16[1,256,512]{2,1,0:T(8,128)(2,1)}), bf16[1,256,2048]{2,1,0:T(8,128)(2,1)}) %all-gather.7.cloned.1.call-update) | async-done | bytes 1048592 | tf_op jit(solution)/shard_map/all_gather | solution.py:58
  48.6 2.2 slice.913
  50.8 2.2 slice.917
  53.0 2.2 slice.923
  55.2 2.2 slice.936
  120.2 2.8 slice.1070
  123.0 2.8 slice.906
  198.5 2.4 pad.408
  213.9 2.2 pad.406
  218.4 2.4 pad.410
  223.2 2.2 pad.376
  232.4 32.2 %all-gather = f32[32,1,128]{2,1,0:T(1,128)S(1)} all-gather(f32[1,1,128]{2,1,0:T(1,128)S(1)} %bitcast.235), channel_id=1, replica_groups=mesh['seq'=32,'batch'=4,'state'=4] {'seq'}, dimensions={0}, use_global_device_ids=true | all-gather | bytes 16896 | tf_op jit(solution)/shard_map/all_gather | solution.py:11
  264.5 27.9 %all-gather.1 = f32[32,1,128]{2,1,0:T(1,128)S(1)} all-gather(f32[1,1,128]{2,1,0:T(1,128)S(1)} %bitcast.234), channel_id=1, replica_groups=mesh['seq'=32,'batch'=4,'state'=4] {'seq'}, dimensions={0}, use_global_device_ids=true | all-gather | bytes 16896 | tf_op jit(solution)/shard_map/all_gather | solution.py:11
  292.5 28.4 %all-gather.2 = f32[32,1,128]{2,1,0:T(1,128)S(1)} all-gather(f32[1,1,128]{2,1,0:T(1,128)S(1)} %bitcast.233), channel_id=1, replica_groups=mesh['seq'=32,'batch'=4,'state'=4] {'seq'}, dimensions={0}, use_global_device_ids=true | all-gather | bytes 16896 | tf_op jit(solution)/shard_map/all_gather | solution.py:11
  320.9 27.4 %all-gather.3 = f32[32,1,128]{2,1,0:T(1,128)S(1)} all-gather(f32[1,1,128]{2,1,0:T(1,128)S(1)} %bitcast.232), channel_id=1, replica_groups=mesh['seq'=32,'batch'=4,'state'=4] {'seq'}, dimensions={0}, use_global_device_ids=true | all-gather | bytes 16896 | tf_op jit(solution)/shard_map/all_gather | solution.py:11
  358.8 245.4 %psum.15 = f32[2,128]{1,0:T(2,128)S(1)} all-reduce(f32[2,128]{1,0:T(2,128)S(1)} %pad_maximum_fusion.50), channel_id=1, replica_groups=mesh['seq'=32,'batch'=4,'state'=4] {'seq','batch'}, use_global_device_ids=true, to_apply=%region_7.8 | all-reduce | flops 256 | bytes 2048 | tf_op jit(solution)/shard_map/psum | solution.py:129
  604.8 96.5 %all-reduce.118.cloned.1.call-done = f32[2,2048,128]{1,2,0:T(8,128)} async-done(((f32[2,2048,128]{1,2,0:T(8,128)}), f32[2,2048,128]{1,2,0:T(8,128)}) %all-reduce.118.cloned.1.call-update) | async-done | bytes 2097168 | tf_op jit(solution)/shard_map/psum | solution.py:129
  703.5 36.2 %reduce-scatter.2.cloned.1.call-done = f32[512,256]{0,1:T(8,128)} async-done(((f32[2048,256]{0,1:T(8,128)}), f32[512,256]{0,1:T(8,128)}) %reduce-scatter.2.cloned.1.call-update) | async-done | bytes 524304 | tf_op jit(solution)/shard_map/reduce_scatter | solution.py:111
  (613 shorter events, 188.3 us)
Async XLA Ops:
  7.2 218.7 %copy-start = (bf16[2,2048,128]{2,1,0:T(8,128)(2,1)S(1)}, bf16[2,2048,128]{2,1,0:T(8,128)(2,1)}, u32[]{:S(2)}) copy-start(bf16[2,2048,128]{2,1,0:T(8,128)(2,1)} %param.16) | copy-start | bytes 3145732
  7.2 17.9 %copy-start.36 = (s32[1,256]{1,0:T(1,128)S(1)}, s32[1,256]{1,0:T(1,128)}, u32[]{:S(2)}) copy-start(s32[1,256]{1,0:T(1,128)} %param.14) | copy-start | bytes 3076
  7.2 18.4 %copy-start.29 = (f32[1,256]{1,0:T(1,128)S(1)}, f32[1,256]{1,0:T(1,128)}, u32[]{:S(2)}) copy-start(f32[1,256]{1,0:T(1,128)} %param.13) | copy-start | bytes 3076
  7.2 39.0 %all-gather.7.cloned.1.call-start = ((), (), s32[]{:S(2)}) async-start(), calls=%async_computation.1 | async-start | bytes 1310720 | tf_op jit(solution)/shard_map/all_gather | solution.py:58
  7.9 24.9 %copy-start.35 = (f32[1,4,2,128]{3,2,1,0:T(2,128)S(1)}, f32[1,4,2,128]{3,2,1,0:T(2,128)}, u32[]{:S(2)}) copy-start(f32[1,4,2,128]{3,2,1,0:T(2,128)} %param.18) | copy-start | bytes 12292
  7.9 24.9 %copy-start.37 = (s32[1,4]{1,0:T(1,128)S(1)}, s32[1,4]{1,0:T(1,128)}, u32[]{:S(2)}) copy-start(s32[1,4]{1,0:T(1,128)} %param.19) | copy-start | bytes 52
  8.0 38.2 %copy-start.2 = (bf16[2,2048,128]{2,1,0:T(8,128)(2,1)S(1)}, bf16[2,2048,128]{2,1,0:T(8,128)(2,1)}, u32[]{:S(2)}) copy-start(bf16[2,2048,128]{2,1,0:T(8,128)(2,1)} %param.17) | copy-start | bytes 3145732
  8.0 217.9 %all-gather.9.cloned.1.call-start = ((), (), s32[]{:S(2)}) async-start(), calls=%async_computation.3 | async-start | bytes 1310720 | tf_op jit(solution)/shard_map/all_gather | solution.py:57
  8.7 692.6 %all-reduce.118.cloned.1.call-start = ((), (), s32[]{:S(2)}) async-start(), calls=%async_computation.4 | async-start | bytes 4194304 | tf_op jit(solution)/shard_map/psum | solution.py:129
  9.5 20.7 %copy-start.31 = (f32[128]{0:T(128)}, f32[128]{0:T(128)S(1)}, u32[]{:S(2)}) copy-start(f32[128]{0:T(128)S(1)} %get-tuple-element.410) | copy-start | bytes 1540
  9.5 20.7 %copy-start.32 = (f32[128]{0:T(128)}, f32[128]{0:T(128)S(1)}, u32[]{:S(2)}) copy-start(f32[128]{0:T(128)S(1)} %get-tuple-element.411) | copy-start | bytes 1540
  97.4 35.3 %copy-start.26 = (f32[1,128]{0,1:T(8,128)S(1)}, f32[1,128]{0,1:T(8,128)}, u32[]{:S(2)}) copy-start(f32[1,128]{0,1:T(8,128)} %get-tuple-element.328) | copy-start | bytes 1540
  97.4 35.4 %copy-start.25 = (f32[1,128]{0,1:T(8,128)S(1)}, f32[1,128]{0,1:T(8,128)}, u32[]{:S(2)}) copy-start(f32[1,128]{0,1:T(8,128)} %get-tuple-element.325) | copy-start | bytes 1540
  97.4 35.5 %copy-start.27 = (f32[1,128]{0,1:T(8,128)S(1)}, f32[1,128]{0,1:T(8,128)}, u32[]{:S(2)}) copy-start(f32[1,128]{0,1:T(8,128)} %get-tuple-element.358) | copy-start | bytes 1540
  146.8 17.4 %copy-start.21 = (f32[7,128]{0,1:T(8,128)S(1)}, f32[7,128]{0,1:T(8,128)}, u32[]{:S(2)}) copy-start(f32[7,128]{0,1:T(8,128)} %slice.1012) | copy-start | bytes 10756
  146.8 17.4 %copy-start.22 = (f32[7,128]{0,1:T(8,128)S(1)}, f32[7,128]{0,1:T(8,128)}, u32[]{:S(2)}) copy-start(f32[7,128]{0,1:T(8,128)} %slice.965) | copy-start | bytes 10756
  164.2 18.4 %copy-start.9 = (f32[15,128]{0,1:T(8,128)S(1)}, f32[15,128]{0,1:T(8,128)}, u32[]{:S(2)}) copy-start(f32[15,128]{0,1:T(8,128)} %slice.1017) | copy-start | bytes 23044
  164.2 18.4 %copy-start.10 = (f32[15,128]{0,1:T(8,128)S(1)}, f32[15,128]{0,1:T(8,128)}, u32[]{:S(2)}) copy-start(f32[15,128]{0,1:T(8,128)} %slice.954) | copy-start | bytes 23044
  165.0 18.2 %copy-start.20 = (f32[15,128]{0,1:T(8,128)S(1)}, f32[15,128]{0,1:T(8,128)}, u32[]{:S(2)}) copy-start(f32[15,128]{0,1:T(8,128)} %slice.1024) | copy-start | bytes 23044
  175.3 12.1 %copy-start.7 = (f32[31,128]{0,1:T(8,128)S(1)}, f32[31,128]{0,1:T(8,128)}, u32[]{:S(2)}) copy-start(f32[31,128]{0,1:T(8,128)} %slice.1022) | copy-start | bytes 47620
  175.3 12.1 %copy-start.8 = (f32[31,128]{0,1:T(8,128)S(1)}, f32[31,128]{0,1:T(8,128)}, u32[]{:S(2)}) copy-start(f32[31,128]{0,1:T(8,128)} %slice.943) | copy-start | bytes 47620
  175.4 12.1 %copy-start.18 = (f32[31,128]{0,1:T(8,128)S(1)}, f32[31,128]{0,1:T(8,128)}, u32[]{:S(2)}) copy-start(f32[31,128]{0,1:T(8,128)} %slice.1029) | copy-start | bytes 47620
  190.2 13.5 %copy-start.23 = (f32[16,128]{0,1:T(8,128)S(1)}, f32[16,128]{0,1:T(8,128)}, u32[]{:S(2)}) copy-start(f32[16,128]{0,1:T(8,128)} %add.872) | copy-start | bytes 24580
  356.9 382.8 %reduce-scatter.2.cloned.1.call-start = ((), (), s32[]{:S(2)}) async-start(), calls=%async_computation.2 | async-start | bytes 2621440 | tf_op jit(solution)/shard_map/reduce_scatter | solution.py:111
  (18 other events, 110.0 us)
Sparse Core Ops, SparseCore 0:
  10.1 36.0 all-gather.6
  48.3 32.0 all-gather.8
  357.0 344.2 all-reduce.117
  704.3 35.3 reduce-scatter.1
where the time goes:
time: 760 us; the launch traced here: 748 us
  blocking collectives  361 us (48%)
  local copies, waits for them, and re-layouts  181 us (24%)
  waiting for transfers between devices  147 us (19%)
  other arithmetic  34 us (4%)
  between operations  16.7 us (2%)
    psum x1, blocking collectives, local(): lax.psum((partial_proj, partial_decay), ('seq', 'batch'))  245 us
    all_gather x4, blocking collectives, prefix(): pieces = jax.tree.map(lambda part: lax.all_gather(part, axis), value)  116 us
    psum x1, waiting for transfers between devices, local(): lax.psum((partial_proj, partial_decay), ('seq', 'batch'))  96.5 us
    slice x95, local copies, waits for them, and re-layouts, local(): lax.associative_scan(backward_combine, (next_re, next_im, inject_re, inje...  86.7 us
    pad x56, local copies, waits for them, and re-layouts, local(): lax.associative_scan(backward_combine, (next_re, next_im, inject_re, inje...  50.3 us
    reduce_scatter x1, waiting for transfers between devices, local(): lax.psum_scatter(jnp.einsum('khp,ktp->ht', in_proj, adjoint_bf, preferred...  36.2 us
  transfers between devices with their start and end apart: 4, of which 3 were waited for; matrix products, arithmetic and copies ran while one was open for 28% of the time, Pallas kernels for 0%

commit v1 on v0

v1 whole, which is shorter than its diff:
```python
import functools
import math

import jax
import jax.numpy as jnp
from jax import lax
from jax.experimental import pallas as pl
from jax.experimental.pallas import tpu as pltpu
from jax.sharding import PartitionSpec as P

MESH = pl.DeviceIdType.MESH
F32 = jnp.float32
BF16 = jnp.bfloat16
GROUPS = 8
SUMMARY, DECAY, REDUCE, SPREAD = range(4)
PAIR_SUMMARY, PAIR_ADJOINT, PAIR_PROJ, PAIR_DECAY, PAIR_INPUTS = range(5)


def complex_times(left_re, left_im, right_re, right_im):
    return (left_re * right_re - left_im * right_im, left_re * right_im + left_im * right_re)


def conj_times(left_re, left_im, right_re, right_im):
    return (left_re * right_re + left_im * right_im, left_re * right_im - left_im * right_re)


def dot(left, right, left_dim, right_dim):
    return lax.dot_general(
        left, right, (((left_dim,), (right_dim,)), ((), ())), preferred_element_type=F32
    )


def small_exp(x):
    total = jnp.full_like(x, 1.0 / 5040.0)
    for factor in (1.0 / 720.0, 1.0 / 120.0, 1.0 / 24.0, 1.0 / 6.0, 0.5):
        total = total * x + factor
    near = 1.0 + (x + x * x * total)
    return jnp.where(x > -0.4, near, jnp.exp(x))


def cos_sin(angle):
    turns = jnp.floor(angle * (2.0 / math.pi) + 0.5)
    rest = angle - turns * 1.5703125
    rest = rest - turns * 4.837512969970703125e-4
    rest = rest - turns * 7.54978995489188216e-8
    square = rest * rest
    sine = ((-1.9515295891e-4 * square + 8.3321608736e-3) * square - 1.6666654611e-1) * square
    sine = sine * rest + rest
    cosine = (2.443315711809948e-5 * square - 1.388731625493765e-3) * square + 4.166664568298827e-2
    cosine = cosine * square * square - 0.5 * square + 1.0
    half = jnp.floor(turns * 0.5)
    odd = turns - 2.0 * half
    negative = half - 2.0 * jnp.floor(half * 0.5)
    sign = 1.0 - 2.0 * negative
    swap = odd > 0.5
    return (
        sign * jnp.where(swap, -sine, cosine),
        sign * jnp.where(swap, cosine, sine),
    )


def column(row):
    steps = row.shape[1]
    return jnp.concatenate(
        [
            jnp.broadcast_to(row[:, at : at + 128], (128, 128)).T
            for at in range(0, steps, 128)
        ],
        axis=0,
    )


def kernel(
    sizes,
    cot_ref,
    inp_ref,
    step_ref,
    resets_ref,
    rate_ref,
    w_in_ref,
    w_out_ref,
    saved_ref,
    index_ref,
    gi_ref,
    gp_ref,
    gd_ref,
    cot_all,
    inp_all,
    w_in,
    w_out,
    inp_t,
    dec_re,
    dec_im,
    step_col,
    inj_re,
    inj_im,
    drv_re,
    drv_im,
    adj_re,
    adj_im,
    left_re,
    left_im,
    pri_re,
    pri_im,
    adj_bf,
    adj_send,
    adj_cat,
    pair_sum,
    z_sum,
    gi_send,
    gi_recv,
    gi_own,
    gi_bf,
    y_send,
    y_recv,
    z_own,
    z_send,
    z_recv,
    gp_bf,
    z_dec,
    y_dec,
    pair_dec,
    local_sem,
    ring_send,
    ring_recv,
    pair_send,
    pair_recv,
    zs_send,
    zs_recv,
    ys_send,
    ys_recv,
    yd_send,
    yd_recv,
    gi_ssem,
    gi_rsem,
):
    seqs, batches, blocks = sizes
    chips = seqs // 2
    steps, width = cot_all.shape[1], cot_all.shape[2]
    half = steps // 2
    length = steps // GROUPS
    states = dec_re.shape[1]
    rows = y_recv.shape[1]
    piece = z_recv.shape[1]
    s, b, x = lax.axis_index("seq"), lax.axis_index("batch"), lax.axis_index("state")
    z, c = s // 2, s % 2
    partner = {"seq": 2 * z + (1 - c)}
    right, left = (x + 1) % blocks, (x + blocks - 1) % blocks
    across = (x + 2) % blocks

    def chip(offset):
        return {"seq": 2 * ((z + offset) % chips) + c}

    def row(offset):
        return {"batch": (b + offset) % batches}

    def block(offset):
        return {"state": (x + offset) % blocks}

    def remote(src, dst, send, recv, device):
        return pltpu.make_async_remote_copy(
            src_ref=src, dst_ref=dst, send_sem=send, recv_sem=recv, device_id=device, device_id_type=MESH
        )

    barrier = pltpu.get_barrier_semaphore()
    peers = [partner]
    peers += [block(i) for i in range(1, blocks)]
    peers += [row(i) for i in range(1, batches)]
    for peer in peers:
        pl.semaphore_signal(barrier, inc=1, device_id=peer, device_id_type=MESH)

    def greet(i, carry):
        pl.semaphore_signal(barrier, inc=1, device_id=chip(i), device_id_type=MESH)
        return carry

    lax.fori_loop(1, chips, greet, 0)

    def local(src, dst, at):
        copy = pltpu.make_async_copy(src, dst, local_sem.at[at])
        copy.start()
        return copy

    cot_own = local(cot_ref.at[0], cot_all.at[x], 0)
    out_copies = [local(w_out_ref.at[k], w_out.at[:, pl.ds(k * states, states)], 1 + k) for k in range(2)]
    inp_own = local(inp_ref.at[0], inp_all.at[x], 3)
    in_copies = [local(w_in_ref.at[k], w_in.at[:, pl.ds(k * states, states)], 4 + k) for k in range(2)]

    pl.semaphore_wait(barrier, len(peers) + chips - 1)

    low, high = pl.ds(0, half), pl.ds(half, half)

    def ring(ref, whole, at):
        def send(part, device, sem):
            copy = remote(
                ref.at[0, part], whole.at[x, part], ring_send.at[at, sem], ring_recv.at[at, sem], device
            )
            copy.start()
            return copy

        return [
            send(low, block(1), 0),
            send(high, block(blocks - 1), 1),
            send(high, block(1), 2),
            send(low, block(blocks - 1), 3),
        ]

    def forward(whole, at, way):
        owner, part, device = ((left, low, block(1)), (right, high, block(blocks - 1)))[way]
        copy = remote(
            whole.at[owner, part], whole.at[owner, part], ring_send.at[at, 4 + way], ring_recv.at[at, 4 + way], device
        )
        copy.start()
        return copy

    cot_ring = ring(cot_ref, cot_all, 0)

    step = step_ref[...]
    keep = (1 - resets_ref[...]).astype(F32)
    wide = column(step)
    magnitude = column(keep) * small_exp(wide * rate_ref[0:1, :])
    cosine, sine = cos_sin(wide * rate_ref[1:2, :])
    dec_re[...] = magnitude * cosine
    dec_im[...] = magnitude * sine
    step_col[...] = wide

    def part_dot(whole, weights, owner):
        return dot(whole[owner], weights[pl.ds(pl.multiple_of(owner * width, width), width), :], 1, 0)

    cot_own.wait()
    for copy in out_copies:
        copy.wait()
    inject = part_dot(cot_all, w_out, x)
    cot_ring[0].wait_recv()
    cot_on = [forward(cot_all, 0, 0)]
    cot_ring[1].wait_recv()
    cot_on.append(forward(cot_all, 0, 1))
    inp_ring = ring(inp_ref, inp_all, 1)
    cot_ring[2].wait_recv()
    inject += part_dot(cot_all, w_out, left)
    cot_ring[3].wait_recv()
    inject += part_dot(cot_all, w_out, right)
    for copy in cot_on:
        copy.wait_recv()
    inject += part_dot(cot_all, w_out, across)
    inj_re[...] = inject[:, :states]
    inj_im[...] = -inject[:, states:]

    def at_step(j):
        return pl.ds(j, GROUPS, stride=length)

    zero8 = jnp.zeros((GROUPS, states), F32)
    one8 = jnp.ones((GROUPS, states), F32)

    def leave(i, carry):
        prod_re, prod_im, sum_re, sum_im = carry
        at = at_step(length - 1 - i)
        d_re, d_im = dec_re[at, :], dec_im[at, :]
        prod_re, prod_im = conj_times(d_re, d_im, prod_re, prod_im)
        sum_re, sum_im = conj_times(d_re, d_im, inj_re[at, :] + sum_re, inj_im[at, :] + sum_im)
        return prod_re, prod_im, sum_re, sum_im

    grp = lax.fori_loop(0, length, leave, (one8, zero8, zero8, zero8), unroll=True)

    def pass_on(prod_re, prod_im, sum_re, sum_im, at_re, at_im):
        move_re, move_im = complex_times(prod_re, prod_im, at_re, at_im)
        return move_re + sum_re, move_im + sum_im

    def compose(first, then):
        prod_re, prod_im = complex_times(then[0], then[1], first[0], first[1])
        sum_re, sum_im = pass_on(*then, first[2], first[3])
        return prod_re, prod_im, sum_re, sum_im

    grp_rows = [tuple(part[g : g + 1, :] for part in grp) for g in range(GROUPS)]
    own = grp_rows[GROUPS - 1]
    for g in range(GROUPS - 2, -1, -1):
        own = compose(own, grp_rows[g])
    pair_sum[c] = jnp.concatenate(own, axis=0)
    sum_pair = remote(
        pair_sum.at[c], pair_sum.at[c], pair_send.at[PAIR_SUMMARY], pair_recv.at[PAIR_SUMMARY], partner
    )
    sum_pair.start()
    sum_pair.wait_recv()

    def four(ref, at):
        return tuple(ref[at, k : k + 1, :] for k in range(4))

    later = four(pair_sum, 1)
    z_sum[z] = jnp.concatenate(compose(later, four(pair_sum, 0)), axis=0)

    def z_start(src, dst, kind):
        def go(i, carry):
            remote(src(i), dst, zs_send.at[kind], zs_recv.at[kind], chip(i)).start()
            return carry

        lax.fori_loop(1, chips, go, 0)

    def z_all(buffer, kind):
        part = buffer.at[pl.ds(0, chips - 1)]
        return remote(part, part, zs_send.at[kind], zs_recv.at[kind], chip(1))

    z_start(lambda i: z_sum.at[z], z_sum.at[z], SUMMARY)

    inp_ring[0].wait_recv()
    inp_on = [forward(inp_all, 1, 0)]
    inp_ring[1].wait_recv()
    inp_on.append(forward(inp_all, 1, 1))
    inp_own.wait()
    for copy in in_copies:
        copy.wait()
    drive = part_dot(inp_all, w_in, x)

    columns = pl.ds(pl.multiple_of(c * steps, steps), steps)

    def turn(owner, at):
        there = inp_t.at[pl.ds(pl.multiple_of(owner * width, width), width), columns]
        there[...] = inp_all[owner].T
        copy = remote(there, there, pair_send.at[PAIR_INPUTS + at], pair_recv.at[PAIR_INPUTS + at], partner)
        copy.start()
        return copy

    turned = [turn(x, 0)]

    z_all(z_sum, SUMMARY).wait_recv()
    in_re, in_im = jnp.zeros((1, states), F32), jnp.zeros((1, states), F32)
    for j in range(chips - 1, 0, -1):
        next_re, next_im = pass_on(*four(z_sum, j), in_re, in_im)
        in_re, in_im = jnp.where(j > z, next_re, in_re), jnp.where(j > z, next_im, in_im)
    next_re, next_im = pass_on(*later, in_re, in_im)
    in_re, in_im = jnp.where(c == 0, next_re, in_re), jnp.where(c == 0, next_im, in_im)
    enter = [None] * GROUPS
    for g in range(GROUPS - 1, -1, -1):
        enter[g] = (in_re, in_im)
        in_re, in_im = pass_on(*grp_rows[g], in_re, in_im)

    def back(i, carry):
        at = at_step(length - 1 - i)
        a_re, a_im = inj_re[at, :] + carry[0], inj_im[at, :] + carry[1]
        adj_re[at, :] = a_re
        adj_im[at, :] = a_im
        l_re, l_im = conj_times(dec_re[at, :], dec_im[at, :], a_re, a_im)
        left_re[at, :] = l_re
        left_im[at, :] = l_im
        return l_re, l_im

    lax.fori_loop(
        0,
        length,
        back,
        tuple(jnp.concatenate([pair[k] for pair in enter], axis=0) for k in range(2)),
        unroll=True,
    )
    bf_re, bf_im = adj_re[...].astype(BF16), adj_im[...].astype(BF16)
    adj_bf[:, :states] = bf_re
    adj_bf[:, states:] = bf_im
    first = (jnp.zeros((steps, states), jnp.int32) + c) == 0
    own_rows = pl.ds(pl.multiple_of(c * steps, steps), steps)
    adj_send[...] = jnp.where(first, adj_im[...], adj_re[...]).astype(BF16)
    adj_cat[own_rows, :] = jnp.where(first, adj_re[...], adj_im[...]).astype(BF16)
    adj_pair = remote(
        adj_send, adj_cat.at[own_rows], pair_send.at[PAIR_ADJOINT], pair_recv.at[PAIR_ADJOINT], partner
    )
    adj_pair.start()

    inp_ring[2].wait_recv()
    turned.append(turn(left, 1))
    inp_ring[3].wait_recv()
    turned.append(turn(right, 2))
    for copy in inp_on:
        copy.wait_recv()
    turned.append(turn(across, 3))

    def gi_part(owner):
        return dot(adj_bf[...], w_in[pl.ds(pl.multiple_of(owner * width, width), width), :], 1, 1)

    gi_copies = []
    for i in range(1, blocks):
        gi_send[i - 1] = gi_part((x + i) % blocks).astype(BF16)
        copy = remote(gi_send.at[i - 1], gi_recv.at[i - 1], gi_ssem.at[i - 1], gi_rsem.at[i - 1], block(i))
        copy.start()
        gi_copies.append(copy)

    adj_pair.wait_recv()
    for copy in turned:
        copy.wait_recv()

    def gp_part(owner):
        return dot(inp_t[pl.ds(pl.multiple_of(owner * rows, rows), rows), :], adj_cat[...], 1, 0)

    y_copies = []
    for i in range(1, batches):
        y_send[i - 1] = gp_part((b + i) % batches).astype(BF16)
        copy = remote(y_send.at[i - 1], y_recv.at[i - 1], ys_send.at[i - 1], ys_recv.at[i - 1], row(i))
        copy.start()
        y_copies.append(copy)
    gp_own = gp_part(b)
    z_own[...] = gp_own

    for owner in (left, right, across):
        drive += part_dot(inp_all, w_in, owner)
    drv_re[...] = drive[:, :states]
    drv_im[...] = drive[:, states:]

    def run(i, carry):
        prod_re, prod_im, sum_re, sum_im = carry
        at = at_step(i)
        d_re, d_im = dec_re[at, :], dec_im[at, :]
        prod_re, prod_im = complex_times(d_re, d_im, prod_re, prod_im)
        sum_re, sum_im = pass_on(d_re, d_im, drv_re[at, :], drv_im[at, :], sum_re, sum_im)
        return prod_re, prod_im, sum_re, sum_im

    fwd = lax.fori_loop(0, length, run, (one8, zero8, zero8, zero8), unroll=True)
    fwd_rows = [tuple(part[g : g + 1, :] for part in fwd) for g in range(GROUPS)]
    spans = saved_ref.shape[1]
    begin = [None] * GROUPS
    for span in range(spans):
        slot = jnp.zeros((1, states), jnp.int32) + index_ref[0, span]
        at_re, at_im = jnp.zeros((1, states), F32), jnp.zeros((1, states), F32)
        for k in range(spans):
            at_re = jnp.where(slot == k, saved_ref[0, k, 0:1, :], at_re)
            at_im = jnp.where(slot == k, saved_ref[0, k, 1:2, :], at_im)
        for g in range(span * GROUPS // spans, (span + 1) * GROUPS // spans):
            begin[g] = (at_re, at_im)
            at_re, at_im = pass_on(*fwd_rows[g], at_re, at_im)

    def rerun(i, carry):
        at = at_step(i)
        pri_re[at, :] = carry[0]
        pri_im[at, :] = carry[1]
        return pass_on(dec_re[at, :], dec_im[at, :], drv_re[at, :], drv_im[at, :], *carry)

    lax.fori_loop(
        0,
        length,
        rerun,
        tuple(jnp.concatenate([pair[k] for pair in begin], axis=0) for k in range(2)),
        unroll=True,
    )
    wide_re, wide_im = conj_times(pri_re[...], pri_im[...], left_re[...], left_im[...])
    weight = step_col[...]
    z_dec[z] = jnp.concatenate(
        [jnp.sum(weight * part, axis=0, keepdims=True) for part in (wide_re, wide_im)], axis=0
    )
    z_start(lambda i: z_dec.at[z], z_dec.at[z], DECAY)

    for copy in y_copies:
        copy.wait_recv()
    total = z_own[...]
    for i in range(batches - 1):
        total += y_recv[i].astype(F32)
    z_own[...] = total
    z_send[...] = total.reshape(chips, piece, states).astype(BF16)
    z_recv[z] = jnp.zeros((piece, states), BF16)
    z_start(lambda i: z_send.at[(z + i) % chips], z_recv.at[z], REDUCE)

    z_all(z_dec, DECAY).wait_recv()
    part = z_dec[0]
    for j in range(1, chips):
        part += z_dec[j]
    y_dec[b] = part
    dec_copies = []
    for i in range(1, batches):
        copy = remote(y_dec.at[b], y_dec.at[b], yd_send.at[i - 1], yd_recv.at[i - 1], row(i))
        copy.start()
        dec_copies.append(copy)

    own_gi = gi_part(x)
    for i in range(blocks - 1):
        gi_copies[i].wait_recv()
        own_gi += gi_recv[i].astype(F32)
    gi_bf[...] = own_gi.astype(BF16)
    gi_out = local(gi_bf, gi_ref.at[0], 6)

    z_all(z_recv, REDUCE).wait_recv()
    total = z_own[pl.ds(pl.multiple_of(z * piece, piece), piece), :]
    for j in range(chips):
        total += z_recv[j].astype(F32)
    scale = 1.0 / math.sqrt(batches * seqs * steps)
    gp_bf[c, z] = (total * scale).astype(BF16)
    z_start(lambda i: gp_bf.at[c, z], gp_bf.at[c, z], SPREAD)

    for copy in dec_copies:
        copy.wait_recv()
    part = y_dec[0]
    for j in range(1, batches):
        part += y_dec[j]
    pair_dec[c] = part
    dec_pair = remote(pair_dec.at[c], pair_dec.at[c], pair_send.at[PAIR_DECAY], pair_recv.at[PAIR_DECAY], partner)
    dec_pair.start()
    dec_pair.wait_recv()
    gd_ref[...] = (pair_dec[0] + pair_dec[1]) / (batches * seqs * steps)

    z_all(gp_bf.at[c], SPREAD).wait_recv()
    gp_pair = remote(gp_bf.at[c], gp_bf.at[c], pair_send.at[PAIR_PROJ], pair_recv.at[PAIR_PROJ], partner)
    gp_pair.start()
    gp_pair.wait_recv()
    gp_out = local(gp_bf, gp_ref, 7)

    for copy in cot_ring + cot_on + inp_ring + inp_on + turned + gi_copies + y_copies + dec_copies:
        copy.wait_send()
    for copy in (sum_pair, adj_pair, dec_pair, gp_pair):
        copy.wait_send()
    for buffer, kind in ((z_sum, SUMMARY), (z_dec, DECAY), (z_send, REDUCE), (gp_bf.at[c], SPREAD)):
        z_all(buffer, kind).wait_send()
    gi_out.wait()
    gp_out.wait()


def local(sizes, inputs, cotangent, step_size, resets, log_decay, in_proj, out_proj, saved_states, saved_index):
    seqs, batches, blocks = sizes
    chips = seqs // 2
    _, steps, width = inputs.shape
    _, features, states = in_proj.shape
    rows = features // batches
    piece = rows // chips
    any_spec = pl.BlockSpec(memory_space=pl.ANY)
    vmem_spec = pl.BlockSpec(memory_space=pltpu.VMEM)
    per_step = pltpu.VMEM((steps, states), F32)
    dma = pltpu.SemaphoreType.DMA
    grad_inputs, grad_proj, grad_decay = pl.pallas_call(
        functools.partial(kernel, sizes),
        out_shape=(
            jax.ShapeDtypeStruct((1, steps, width), BF16),
            jax.ShapeDtypeStruct((2, chips, piece, states), BF16),
            jax.ShapeDtypeStruct((2, states), F32),
        ),
        in_specs=[
            any_spec,
            any_spec,
            vmem_spec,
            vmem_spec,
            vmem_spec,
            any_spec,
            any_spec,
            vmem_spec,
            pl.BlockSpec(memory_space=pltpu.SMEM),
        ],
        out_specs=(any_spec, any_spec, vmem_spec),
        scratch_shapes=[
            pltpu.VMEM((blocks, steps, width), BF16),
            pltpu.VMEM((blocks, steps, width), BF16),
            pltpu.VMEM((features, 2 * states), BF16),
            pltpu.VMEM((features, 2 * states), BF16),
            pltpu.VMEM((features, 2 * steps), BF16),
            *([per_step] * 13),
            pltpu.VMEM((steps, 2 * states), BF16),
            pltpu.VMEM((steps, states), BF16),
            pltpu.VMEM((2 * steps, states), BF16),
            pltpu.VMEM((2, 4, states), F32),
            pltpu.VMEM((chips, 4, states), F32),
            pltpu.VMEM((blocks - 1, steps, width), BF16),
            pltpu.VMEM((blocks - 1, steps, width), BF16),
            pltpu.VMEM((steps, width), F32),
            pltpu.VMEM((steps, width), BF16),
            pltpu.VMEM((batches - 1, rows, states), BF16),
            pltpu.VMEM((batches - 1, rows, states), BF16),
            pltpu.VMEM((rows, states), F32),
            pltpu.VMEM((chips, piece, states), BF16),
            pltpu.VMEM((chips, piece, states), BF16),
            pltpu.VMEM((2, chips, piece, states), BF16),
            pltpu.VMEM((chips, 2, states), F32),
            pltpu.VMEM((batches, 2, states), F32),
            pltpu.VMEM((2, 2, states), F32),
            dma((8,)),
            dma((2, 6)),
            dma((2, 6)),
            dma((PAIR_INPUTS + blocks,)),
            dma((PAIR_INPUTS + blocks,)),
            dma((4,)),
            dma((4,)),
            dma((batches - 1,)),
            dma((batches - 1,)),
            dma((batches - 1,)),
            dma((batches - 1,)),
            dma((blocks - 1,)),
            dma((blocks - 1,)),
        ],
        compiler_params=pltpu.CompilerParams(
            collective_id=0, has_side_effects=True, vmem_limit_bytes=40 * 1024 * 1024
        ),
    )(cotangent, inputs, step_size, resets, log_decay, in_proj, out_proj, saved_states, saved_index)
    return (grad_inputs, grad_proj.reshape(2, rows, states).astype(F32), grad_decay)


def solution(mesh):
    in_specs = (
        P("batch", "seq", "state"),
        P("batch", "seq", "state"),
        P("batch", "seq"),
        P("batch", "seq"),
        P(None, "state"),
        P(None, None, "state"),
        P(None, None, "state"),
        P("batch", "seq", None, "state"),
        P("batch", "seq"),
    )
    out_specs = (P("batch", "seq", "state"), P(None, "batch", "state"), P(None, "state"))
    sizes = (mesh.shape["seq"], mesh.shape["batch"], mesh.shape["state"])
    return jax.shard_map(
        functools.partial(local, sizes), mesh=mesh, in_specs=in_specs, out_specs=out_specs, check_vma=False
    )
```

time: 760 us -> 80.5 us (0.11); the launches traced: 748 us -> 80.1 us
  blocking collectives: 361 us -> 0 us
  local copies, waits for them, and re-layouts: 181 us -> 8.98 us
  waiting for transfers between devices: 147 us -> 0 us
  Pallas kernels: 0 us -> 69.6 us
  other arithmetic: 34 us -> 0.85 us
  between operations: 16.7 us -> 0.66 us
    psum x1 -> x0, blocking collectives: 245 us -> none  [local(): lax.psum((partial_proj, partial_decay), ('seq', 'batch'))]
    all_gather x4 -> x0, blocking collectives: 116 us -> none  [prefix(): pieces = jax.tree.map(lambda part: lax.all_gather(part, axis), value)]
    psum x1 -> x0, waiting for transfers between devices: 96.5 us -> none  [local(): lax.psum((partial_proj, partial_decay), ('seq', 'batch'))]
    slice x179 -> x0, local copies, waits for them, and re-layouts: 91.9 us -> none  [the longest x95 86.7 us: local(): lax.associative_scan(backward_combine, (next_re, next_im, inject_re, inje...]
    pallas_call x0 -> x1, Pallas kernels: none -> 69.6 us  [local(): pl.pallas_call(functools.partial(kernel, sizes), out_shape=(jax.ShapeDtyp...]
    pad x92 -> x0, local copies, waits for them, and re-layouts: 51.7 us -> none  [the longest x56 50.3 us: local(): lax.associative_scan(backward_combine, (next_re, next_im, inject_re, inje...]
    reduce_scatter x1 -> x0, waiting for transfers between devices: 36.2 us -> none  [local(): lax.psum_scatter(jnp.einsum('khp,ktp->ht', in_proj, adjoint_bf, preferred...]
    mul x26 -> x0, local copies, waits for them, and re-layouts: 20.7 us -> none  [the longest x6 5.51 us: complex_times(): left_im * right_im]
  transfers between devices with their start and end apart: 4 -> 0, of which waited for: 3 -> 0; matrix products, arithmetic and copies ran while one was open for 28% -> 0% of each run, Pallas kernels for 0% -> 0%
where the time goes in v1:
time: 80.5 us; the launch traced here: 80.1 us
  Pallas kernels  69.6 us (86%)
  local copies, waits for them, and re-layouts  8.98 us (11%)
  other arithmetic  0.85 us (1%)
    pallas_call x1, Pallas kernels, local(): pl.pallas_call(functools.partial(kernel, sizes), out_shape=(jax.ShapeDtyp...  69.6 us
    unnamed x20, local copies, waits for them, and re-layouts  8.98 us

profile of v1, /device:TPU:1, one launch (start us, length us, event | category | flops | bytes accessed | tf_op | source)
XLA Modules:
  0.0 80.1 jit_solution(6589986195007794781)
XLA Ops:
  0.6 0.0 copy-start
  0.6 1.2 %copy-done = bf16[2,2048,128]{2,1,0:T(8,128)(2,1)S(1)} copy-done((bf16[2,2048,128]{2,1,0:T(8,128)(2,1)S(1)}, bf16[2,2048,128]{2,1,0:T(8,128)(2,1)}, u32[]{:S(2)}) %copy-start) | copy-done | bytes 1048600
  1.9 0.0 copy-start.1
  1.9 1.2 %copy-done.1 = bf16[2,2048,128]{2,1,0:T(8,128)(2,1)S(1)} copy-done((bf16[2,2048,128]{2,1,0:T(8,128)(2,1)S(1)}, bf16[2,2048,128]{2,1,0:T(8,128)(2,1)}, u32[]{:S(2)}) %copy-start.1) | copy-done | bytes 1048600
  3.1 0.0 copy-start.2
  3.1 0.9 %copy-done.2 = bf16[1,256,512]{2,1,0:T(8,128)(2,1)S(1)} copy-done((bf16[1,256,512]{2,1,0:T(8,128)(2,1)S(1)}, bf16[1,256,512]{2,1,0:T(8,128)(2,1)}, u32[]{:S(2)}) %copy-start.2) | copy-done | bytes 262168
  4.0 0.0 copy-start.3
  4.0 0.9 %copy-done.3 = bf16[1,256,512]{2,1,0:T(8,128)(2,1)S(1)} copy-done((bf16[1,256,512]{2,1,0:T(8,128)(2,1)S(1)}, bf16[1,256,512]{2,1,0:T(8,128)(2,1)}, u32[]{:S(2)}) %copy-start.3) | copy-done | bytes 262168
  5.0 0.0 copy-start.4
  5.0 0.7 copy-done.4
  5.7 0.0 copy-start.5
  5.7 0.7 copy-done.5
  6.4 0.0 copy-start.6
  6.4 0.7 copy-done.6
  7.0 0.0 copy-start.7
  7.0 0.7 copy-done.7
  7.7 0.0 copy-start.8
  7.7 0.7 copy-done.8
  8.4 69.6 %shard_map.112 = (bf16[1,256,512]{2,1,0:T(8,128)(2,1)S(1)}, bf16[2,16,32,128]{3,2,1,0:T(8,128)(2,1)S(1)}, f32[2,128]{1,0:T(2,128)S(1)}) custom-call(bf16[1,256,512]{2,1,0:T(8,128)(2,1)S(1)} %copy-done.2, bf16[1,256,512]{2,1,0:T(8,128)(2,1)S(1)} %copy-done.3, f32[1,256]{1,0:T(1,128)S(1)} %copy-done.5, s32[1,256]{1,0:T(1,128)S(1)} %copy-done.6, ...), custom_call_target="tpu_custom_call" | custom-call | tf_op jit(solution)/shard_map/pallas_call | solution.py:519
  78.0 0.8 %bitcast_convert_fusion = f32[2,512,128]{2,1,0:T(8,128)} fusion(bf16[2,16,32,128]{3,2,1,0:T(8,128)(2,1)S(1)} %get-tuple-element.7), kind=kLoop, calls=%fused_computation | loop fusion | flops 131072 | bytes 786432 | tf_op jit(solution)/shard_map/convert_element_type | solution.py:581
  78.9 0.7 copy.14
  79.6 0.6 copy.15
Async XLA Ops:
  0.6 1.2 %copy-start = (bf16[2,2048,128]{2,1,0:T(8,128)(2,1)S(1)}, bf16[2,2048,128]{2,1,0:T(8,128)(2,1)}, u32[]{:S(2)}) copy-start(bf16[2,2048,128]{2,1,0:T(8,128)(2,1)} %w_in_ref.1) | copy-start | bytes 3145732
  1.9 1.2 %copy-start.1 = (bf16[2,2048,128]{2,1,0:T(8,128)(2,1)S(1)}, bf16[2,2048,128]{2,1,0:T(8,128)(2,1)}, u32[]{:S(2)}) copy-start(bf16[2,2048,128]{2,1,0:T(8,128)(2,1)} %w_out_ref.1) | copy-start | bytes 3145732
  3.1 0.9 %copy-start.2 = (bf16[1,256,512]{2,1,0:T(8,128)(2,1)S(1)}, bf16[1,256,512]{2,1,0:T(8,128)(2,1)}, u32[]{:S(2)}) copy-start(bf16[1,256,512]{2,1,0:T(8,128)(2,1)} %cot_ref.1) | copy-start | bytes 786436
  4.0 0.9 %copy-start.3 = (bf16[1,256,512]{2,1,0:T(8,128)(2,1)S(1)}, bf16[1,256,512]{2,1,0:T(8,128)(2,1)}, u32[]{:S(2)}) copy-start(bf16[1,256,512]{2,1,0:T(8,128)(2,1)} %inp_ref.1) | copy-start | bytes 786436
  5.0 0.7 copy-start.4
  5.7 0.7 copy-start.5
  6.4 0.7 copy-start.6
  7.0 0.7 copy-start.7
  7.7 0.7 copy-start.8

commit v2 on v1

--- a/solution.py
+++ b/solution.py
@@ -13,7 +13,7 @@
 BF16 = jnp.bfloat16
 GROUPS = 8
 SUMMARY, DECAY, REDUCE, SPREAD = range(4)
-PAIR_SUMMARY, PAIR_ADJOINT, PAIR_PROJ, PAIR_DECAY, PAIR_INPUTS = range(5)
+PAIR_ADJOINT, PAIR_PROJ, PAIR_DECAY, PAIR_INPUTS = range(4)
 
 
 def complex_times(left_re, left_im, right_re, right_im):
@@ -74,13 +74,13 @@
     sizes,
     cot_ref,
     inp_ref,
-    step_ref,
-    resets_ref,
-    rate_ref,
+    step_hbm,
+    resets_hbm,
+    rate_hbm,
     w_in_ref,
     w_out_ref,
-    saved_ref,
-    index_ref,
+    saved_hbm,
+    index_hbm,
     gi_ref,
     gp_ref,
     gd_ref,
@@ -105,11 +105,9 @@
     adj_bf,
     adj_send,
     adj_cat,
-    pair_sum,
     z_sum,
     gi_send,
     gi_recv,
-    gi_own,
     gi_bf,
     y_send,
     y_recv,
@@ -120,6 +118,13 @@
     z_dec,
     y_dec,
     pair_dec,
+    step_ref,
+    resets_ref,
+    rate_ref,
+    saved_ref,
+    index_ref,
+    gd_own,
+    known_sem,
     local_sem,
     ring_send,
     ring_recv,
@@ -148,8 +153,8 @@
     right, left = (x + 1) % blocks, (x + blocks - 1) % blocks
     across = (x + 2) % blocks
 
-    def chip(offset):
-        return {"seq": 2 * ((z + offset) % chips) + c}
+    def chip(offset, core=c):
+        return {"seq": 2 * ((z + offset) % chips) + core}
 
     def row(offset):
         return {"batch": (b + offset) % batches}
@@ -166,14 +171,23 @@
     peers = [partner]
     peers += [block(i) for i in range(1, blocks)]
     peers += [row(i) for i in range(1, batches)]
-    for peer in peers:
-        pl.semaphore_signal(barrier, inc=1, device_id=peer, device_id_type=MESH)
-
-    def greet(i, carry):
-        pl.semaphore_signal(barrier, inc=1, device_id=chip(i), device_id_type=MESH)
-        return carry
-
-    lax.fori_loop(1, chips, greet, 0)
+    peers += [chip(1), chip(chips - 1)]
+
+    def greet(semaphore, devices):
+        for device in devices:
+            pl.semaphore_signal(semaphore, inc=1, device_id=device, device_id_type=MESH)
+
+    greet(barrier, peers)
+
+    rounds = [1 << i for i in range(chips.bit_length() - 2)]
+
+    def round_start(at):
+        if at < len(rounds):
+            greet(known_sem.at[at], [chip(rounds[at]), chip(chips - rounds[at])])
+
+    def round_end(at):
+        if at < len(rounds):
+            pl.semaphore_wait(known_sem.at[at], 2)
 
     def local(src, dst, at):
         copy = pltpu.make_async_copy(src, dst, local_sem.at[at])
@@ -183,9 +197,13 @@
     cot_own = local(cot_ref.at[0], cot_all.at[x], 0)
     out_copies = [local(w_out_ref.at[k], w_out.at[:, pl.ds(k * states, states)], 1 + k) for k in range(2)]
     inp_own = local(inp_ref.at[0], inp_all.at[x], 3)
+    small = ((step_hbm, step_ref), (resets_hbm, resets_ref), (rate_hbm, rate_ref))
+    small_copies = [local(*pair, 8 + k) for k, pair in enumerate(small)]
+    saved_copies = [local(saved_hbm, saved_ref, 11), local(index_hbm, index_ref, 12)]
     in_copies = [local(w_in_ref.at[k], w_in.at[:, pl.ds(k * states, states)], 4 + k) for k in range(2)]
 
-    pl.semaphore_wait(barrier, len(peers) + chips - 1)
+    pl.semaphore_wait(barrier, len(peers))
+    round_start(0)
 
     low, high = pl.ds(0, half), pl.ds(half, half)
 
@@ -214,6 +232,8 @@
 
     cot_ring = ring(cot_ref, cot_all, 0)
 
+    for copy in small_copies:
+        copy.wait()
     step = step_ref[...]
     keep = (1 - resets_ref[...]).astype(F32)
     wide = column(step)
@@ -230,15 +250,21 @@
     for copy in out_copies:
         copy.wait()
     inject = part_dot(cot_all, w_out, x)
+    round_end(0)
+    round_start(1)
     cot_ring[0].wait_recv()
     cot_on = [forward(cot_all, 0, 0)]
     cot_ring[1].wait_recv()
     cot_on.append(forward(cot_all, 0, 1))
     inp_ring = ring(inp_ref, inp_all, 1)
+    round_end(1)
+    round_start(2)
     cot_ring[2].wait_recv()
     inject += part_dot(cot_all, w_out, left)
     cot_ring[3].wait_recv()
     inject += part_dot(cot_all, w_out, right)
+    round_end(2)
+    greet(known_sem.at[3], [partner])
     for copy in cot_on:
         copy.wait_recv()
     inject += part_dot(cot_all, w_out, across)
@@ -274,21 +300,30 @@
     own = grp_rows[GROUPS - 1]
     for g in range(GROUPS - 2, -1, -1):
         own = compose(own, grp_rows[g])
-    pair_sum[c] = jnp.concatenate(own, axis=0)
-    sum_pair = remote(
-        pair_sum.at[c], pair_sum.at[c], pair_send.at[PAIR_SUMMARY], pair_recv.at[PAIR_SUMMARY], partner
-    )
-    sum_pair.start()
-    sum_pair.wait_recv()
+    z_sum[s] = jnp.concatenate(own, axis=0)
+    pl.semaphore_wait(known_sem.at[3], 1)
 
     def four(ref, at):
         return tuple(ref[at, k : k + 1, :] for k in range(4))
 
-    later = four(pair_sum, 1)
-    z_sum[z] = jnp.concatenate(compose(later, four(pair_sum, 0)), axis=0)
+    def far_first(k):
+        return chips // 2 + (k // 2) * (1 - 2 * (k % 2))
+
+    def sum_start(k, carry):
+        for core in range(2):
+            remote(
+                z_sum.at[s], z_sum.at[s], zs_send.at[SUMMARY], zs_recv.at[SUMMARY], chip(far_first(k), core)
+            ).start()
+        return carry
+
+    lax.fori_loop(1, chips, sum_start, 0)
+    remote(z_sum.at[s], z_sum.at[s], zs_send.at[SUMMARY], zs_recv.at[SUMMARY], partner).start()
+    sum_part = z_sum.at[pl.ds(0, seqs - 1)]
+    sum_all = remote(sum_part, sum_part, zs_send.at[SUMMARY], zs_recv.at[SUMMARY], partner)
 
     def z_start(src, dst, kind):
-        def go(i, carry):
+        def go(k, carry):
+            i = far_first(k)
             remote(src(i), dst, zs_send.at[kind], zs_recv.at[kind], chip(i)).start()
             return carry
 
@@ -297,8 +332,6 @@
     def z_all(buffer, kind):
         part = buffer.at[pl.ds(0, chips - 1)]
         return remote(part, part, zs_send.at[kind], zs_recv.at[kind], chip(1))
-
-    z_start(lambda i: z_sum.at[z], z_sum.at[z], SUMMARY)
 
     inp_ring[0].wait_recv()
     inp_on = [forward(inp_all, 1, 0)]
@@ -319,14 +352,21 @@
         return copy
 
     turned = [turn(x, 0)]
-
-    z_all(z_sum, SUMMARY).wait_recv()
+    inp_ring[2].wait_recv()
+    turned.append(turn(left, 1))
+    drive += part_dot(inp_all, w_in, left)
+    inp_ring[3].wait_recv()
+    turned.append(turn(right, 2))
+    drive += part_dot(inp_all, w_in, right)
+    for copy in inp_on:
+        copy.wait_recv()
+    turned.append(turn(across, 3))
+
+    sum_all.wait_recv()
     in_re, in_im = jnp.zeros((1, states), F32), jnp.zeros((1, states), F32)
-    for j in range(chips - 1, 0, -1):
+    for j in range(seqs - 1, 0, -1):
         next_re, next_im = pass_on(*four(z_sum, j), in_re, in_im)
-        in_re, in_im = jnp.where(j > z, next_re, in_re), jnp.where(j > z, next_im, in_im)
-    next_re, next_im = pass_on(*later, in_re, in_im)
-    in_re, in_im = jnp.where(c == 0, next_re, in_re), jnp.where(c == 0, next_im, in_im)
+        in_re, in_im = jnp.where(j > s, next_re, in_re), jnp.where(j > s, next_im, in_im)
     enter = [None] * GROUPS
     for g in range(GROUPS - 1, -1, -1):
         enter[g] = (in_re, in_im)
@@ -361,24 +401,6 @@
     )
     adj_pair.start()
 
-    inp_ring[2].wait_recv()
-    turned.append(turn(left, 1))
-    inp_ring[3].wait_recv()
-    turned.append(turn(right, 2))
-    for copy in inp_on:
-        copy.wait_recv()
-    turned.append(turn(across, 3))
-
-    def gi_part(owner):
-        return dot(adj_bf[...], w_in[pl.ds(pl.multiple_of(owner * width, width), width), :], 1, 1)
-
-    gi_copies = []
-    for i in range(1, blocks):
-        gi_send[i - 1] = gi_part((x + i) % blocks).astype(BF16)
-        copy = remote(gi_send.at[i - 1], gi_recv.at[i - 1], gi_ssem.at[i - 1], gi_rsem.at[i - 1], block(i))
-        copy.start()
-        gi_copies.append(copy)
-
     adj_pair.wait_recv()
     for copy in turned:
         copy.wait_recv()
@@ -395,8 +417,17 @@
     gp_own = gp_part(b)
     z_own[...] = gp_own
 
-    for owner in (left, right, across):
-        drive += part_dot(inp_all, w_in, owner)
+    def gi_part(owner):
+        return dot(adj_bf[...], w_in[pl.ds(pl.multiple_of(owner * width, width), width), :], 1, 1)
+
+    gi_copies = []
+    for i in range(1, blocks):
+        gi_send[i - 1] = gi_part((x + i) % blocks).astype(BF16)
+        copy = remote(gi_send.at[i - 1], gi_recv.at[i - 1], gi_ssem.at[i - 1], gi_rsem.at[i - 1], block(i))
+        copy.start()
+        gi_copies.append(copy)
+
+    drive += part_dot(inp_all, w_in, across)
     drv_re[...] = drive[:, :states]
     drv_im[...] = drive[:, states:]
 
@@ -410,6 +441,8 @@
 
     fwd = lax.fori_loop(0, length, run, (one8, zero8, zero8, zero8), unroll=True)
     fwd_rows = [tuple(part[g : g + 1, :] for part in fwd) for g in range(GROUPS)]
+    for copy in saved_copies:
+        copy.wait()
     spans = saved_ref.shape[1]
     begin = [None] * GROUPS
     for span in range(spans):
@@ -463,13 +496,6 @@
         copy.start()
         dec_copies.append(copy)
 
-    own_gi = gi_part(x)
-    for i in range(blocks - 1):
-        gi_copies[i].wait_recv()
-        own_gi += gi_recv[i].astype(F32)
-    gi_bf[...] = own_gi.astype(BF16)
-    gi_out = local(gi_bf, gi_ref.at[0], 6)
-
     z_all(z_recv, REDUCE).wait_recv()
     total = z_own[pl.ds(pl.multiple_of(z * piece, piece), piece), :]
     for j in range(chips):
@@ -477,6 +503,13 @@
     scale = 1.0 / math.sqrt(batches * seqs * steps)
     gp_bf[c, z] = (total * scale).astype(BF16)
     z_start(lambda i: gp_bf.at[c, z], gp_bf.at[c, z], SPREAD)
+
+    own_gi = gi_part(x)
+    for i in range(blocks - 1):
+        gi_copies[i].wait_recv()
+        own_gi += gi_recv[i].astype(F32)
+    gi_bf[...] = own_gi.astype(BF16)
+    gi_out = local(gi_bf, gi_ref.at[0], 6)
 
     for copy in dec_copies:
         copy.wait_recv()
@@ -487,7 +520,8 @@
     dec_pair = remote(pair_dec.at[c], pair_dec.at[c], pair_send.at[PAIR_DECAY], pair_recv.at[PAIR_DECAY], partner)
     dec_pair.start()
     dec_pair.wait_recv()
-    gd_ref[...] = (pair_dec[0] + pair_dec[1]) / (batches * seqs * steps)
+    gd_own[...] = (pair_dec[0] + pair_dec[1]) / (batches * seqs * steps)
+    gd_out = local(gd_own, gd_ref, 13)
 
     z_all(gp_bf.at[c], SPREAD).wait_recv()
     gp_pair = remote(gp_bf.at[c], gp_bf.at[c], pair_send.at[PAIR_PROJ], pair_recv.at[PAIR_PROJ], partner)
@@ -497,12 +531,12 @@
 
     for copy in cot_ring + cot_on + inp_ring + inp_on + turned + gi_copies + y_copies + dec_copies:
         copy.wait_send()
-    for copy in (sum_pair, adj_pair, dec_pair, gp_pair):
+    for copy in (sum_all, adj_pair, dec_pair, gp_pair):
         copy.wait_send()
-    for buffer, kind in ((z_sum, SUMMARY), (z_dec, DECAY), (z_send, REDUCE), (gp_bf.at[c], SPREAD)):
+    for buffer, kind in ((z_dec, DECAY), (z_send, REDUCE), (gp_bf.at[c], SPREAD)):
         z_all(buffer, kind).wait_send()
-    gi_out.wait()
-    gp_out.wait()
+    for copy in (gi_out, gp_out, gd_out):
+        copy.wait()
 
 
 def local(sizes, inputs, cotangent, step_size, resets, log_decay, in_proj, out_proj, saved_states, saved_index):
@@ -512,8 +546,7 @@
     _, features, states = in_proj.shape
     rows = features // batches
     piece = rows // chips
-    any_spec = pl.BlockSpec(memory_space=pl.ANY)
-    vmem_spec = pl.BlockSpec(memory_space=pltpu.VMEM)
+    hbm_spec = pl.BlockSpec(memory_space=pltpu.HBM)
     per_step = pltpu.VMEM((steps, states), F32)
     dma = pltpu.SemaphoreType.DMA
     grad_inputs, grad_proj, grad_decay = pl.pallas_call(
@@ -523,18 +556,8 @@
             jax.ShapeDtypeStruct((2, chips, piece, states), BF16),
             jax.ShapeDtypeStruct((2, states), F32),
         ),
-        in_specs=[
-            any_spec,
-            any_spec,
-            vmem_spec,
-            vmem_spec,
-            vmem_spec,
-            any_spec,
-            any_spec,
-            vmem_spec,
-            pl.BlockSpec(memory_space=pltpu.SMEM),
-        ],
-        out_specs=(any_spec, any_spec, vmem_spec),
+        in_specs=[hbm_spec] * 9,
+        out_specs=(hbm_spec, hbm_spec, hbm_spec),
         scratch_shapes=[
             pltpu.VMEM((blocks, steps, width), BF16),
             pltpu.VMEM((blocks, steps, width), BF16),
@@ -545,11 +568,9 @@
             pltpu.VMEM((steps, 2 * states), BF16),
             pltpu.VMEM((steps, states), BF16),
             pltpu.VMEM((2 * steps, states), BF16),
-            pltpu.VMEM((2, 4, states), F32),
-            pltpu.VMEM((chips, 4, states), F32),
+            pltpu.VMEM((seqs, 4, states), F32),
             pltpu.VMEM((blocks - 1, steps, width), BF16),
             pltpu.VMEM((blocks - 1, steps, width), BF16),
-            pltpu.VMEM((steps, width), F32),
             pltpu.VMEM((steps, width), BF16),
             pltpu.VMEM((batches - 1, rows, states), BF16),
             pltpu.VMEM((batches - 1, rows, states), BF16),
@@ -560,7 +581,14 @@
             pltpu.VMEM((chips, 2, states), F32),
             pltpu.VMEM((batches, 2, states), F32),
             pltpu.VMEM((2, 2, states), F32),
-            dma((8,)),
+            pltpu.VMEM(step_size.shape, F32),
+            pltpu.VMEM(resets.shape, jnp.int32),
+            pltpu.VMEM(log_decay.shape, F32),
+            pltpu.VMEM(saved_states.shape, F32),
+            pltpu.SMEM(saved_index.shape, jnp.int32),
+            pltpu.VMEM((2, states), F32),
+            pltpu.SemaphoreType.REGULAR((4,)),
+            dma((14,)),
             dma((2, 6)),
             dma((2, 6)),
             dma((PAIR_INPUTS + blocks,)),
@@ -575,7 +603,7 @@
             dma((blocks - 1,)),
         ],
         compiler_params=pltpu.CompilerParams(
-            collective_id=0, has_side_effects=True, vmem_limit_bytes=40 * 1024 * 1024
+            collective_id=0, has_side_effects=True, vmem_limit_bytes=60 * 1024 * 1024
         ),
     )(cotangent, inputs, step_size, resets, log_decay, in_proj, out_proj, saved_states, saved_index)
     return (grad_inputs, grad_proj.reshape(2, rows, states).astype(F32), grad_decay)

time: 80.5 us -> 68.4 us (0.85)
  local copies, waits for them, and re-layouts: 8.98 us -> 1.27 us
  Pallas kernels: 69.6 us -> 64.5 us
  other arithmetic: 0.85 us -> 1.82 us
    unnamed x20 -> x6, local copies, waits for them, and re-layouts: 8.98 us -> 1.27 us
    pallas_call x1, Pallas kernels: 69.6 us -> 64.5 us  [local(): pl.pallas_call(functools.partial(kernel, sizes), out_shape=(jax.ShapeDtyp...]
    convert_element_type x1, other arithmetic: 0.85 us -> 1.82 us  [local(): grad_proj.reshape(2, rows, states).astype(F32)]
where the time goes in v2:
time: 68.4 us; the launch traced here: 68.3 us
  Pallas kernels  64.5 us (94%)
  other arithmetic  1.82 us (3%)
  local copies, waits for them, and re-layouts  1.27 us (2%)
    pallas_call x1, Pallas kernels, local(): pl.pallas_call(functools.partial(kernel, sizes), out_shape=(jax.ShapeDtyp...  64.5 us
    convert_element_type x1, other arithmetic, local(): grad_proj.reshape(2, rows, states).astype(F32)  1.82 us

profile of v2, /device:TPU:1, one launch (start us, length us, event | category | flops | bytes accessed | tf_op | source)
XLA Modules:
  0.0 68.3 jit_solution(17908822491150169064)
XLA Ops:
  0.6 64.5 %shard_map.112 = (bf16[1,256,512]{2,1,0:T(8,128)(2,1)}, bf16[2,16,32,128]{3,2,1,0:T(8,128)(2,1)}, f32[2,128]{1,0:T(2,128)}) custom-call(bf16[1,256,512]{2,1,0:T(8,128)(2,1)} %cot_ref.1, bf16[1,256,512]{2,1,0:T(8,128)(2,1)} %inp_ref.1, f32[1,256]{1,0:T(1,128)} %step_hbm.1, s32[1,256]{1,0:T(1,128)} %resets_hbm.1, f32[2,128]{1,0:T(2,128)} %rate_hbm.1, ...), custom_call_target="tpu_custom_call" | custom-call | tf_op jit(solution)/shard_map/pallas_call | solution.py:552
  65.2 0.0 copy-start
  65.2 1.8 %bitcast_convert_fusion = f32[2,512,128]{2,1,0:T(8,128)} fusion(bf16[2,16,32,128]{3,2,1,0:T(8,128)(2,1)} %get-tuple-element.7), kind=kLoop, calls=%fused_computation | loop fusion | flops 131072 | bytes 786432 | tf_op jit(solution)/shard_map/convert_element_type | solution.py:609
  67.0 0.0 copy-done
  67.0 0.0 copy-start.1
  67.0 0.7 %copy.14 = bf16[1,256,512]{2,1,0:T(8,128)(2,1)} copy(bf16[1,256,512]{2,1,0:T(8,128)(2,1)S(1)} %copy-done) | data formatting | bytes 524288
  67.7 0.0 copy-done.1
  67.7 0.6 copy.15
Async XLA Ops:
  65.2 1.8 %copy-start = (bf16[1,256,512]{2,1,0:T(8,128)(2,1)S(1)}, bf16[1,256,512]{2,1,0:T(8,128)(2,1)}, u32[]{:S(2)}) copy-start(bf16[1,256,512]{2,1,0:T(8,128)(2,1)} %get-tuple-element.12) | copy-start | bytes 786436
  67.0 0.7 %copy-start.1 = (f32[2,128]{1,0:T(2,128)S(1)}, f32[2,128]{1,0:T(2,128)}, u32[]{:S(2)}) copy-start(f32[2,128]{1,0:T(2,128)} %get-tuple-element.14) | copy-start | bytes 3076

commit v3 on v2

--- a/solution.py
+++ b/solution.py
@@ -12,8 +12,8 @@
 F32 = jnp.float32
 BF16 = jnp.bfloat16
 GROUPS = 8
-SUMMARY, DECAY, REDUCE, SPREAD = range(4)
-PAIR_ADJOINT, PAIR_PROJ, PAIR_DECAY, PAIR_INPUTS = range(4)
+SUMMARY, DECAY, REDUCE, NEAR, FAR, OPPOSITE = range(6)
+PAIR_ADJOINT, PAIR_DECAY, PAIR_NEAR, PAIR_FAR, PAIR_INPUTS = range(5)
 
 
 def complex_times(left_re, left_im, right_re, right_im):
@@ -115,6 +115,7 @@
     z_send,
     z_recv,
     gp_bf,
+    gp_f32,
     z_dec,
     y_dec,
     pair_dec,
@@ -358,10 +359,6 @@
     inp_ring[3].wait_recv()
     turned.append(turn(right, 2))
     drive += part_dot(inp_all, w_in, right)
-    for copy in inp_on:
-        copy.wait_recv()
-    turned.append(turn(across, 3))
-
     sum_all.wait_recv()
     in_re, in_im = jnp.zeros((1, states), F32), jnp.zeros((1, states), F32)
     for j in range(seqs - 1, 0, -1):
@@ -400,22 +397,31 @@
         adj_send, adj_cat.at[own_rows], pair_send.at[PAIR_ADJOINT], pair_recv.at[PAIR_ADJOINT], partner
     )
     adj_pair.start()
+    for copy in inp_on:
+        copy.wait_recv()
+    turned.append(turn(across, 3))
 
     adj_pair.wait_recv()
-    for copy in turned:
-        copy.wait_recv()
-
-    def gp_part(owner):
-        return dot(inp_t[pl.ds(pl.multiple_of(owner * rows, rows), rows), :], adj_cat[...], 1, 0)
-
-    y_copies = []
-    for i in range(1, batches):
-        y_send[i - 1] = gp_part((b + i) % batches).astype(BF16)
-        copy = remote(y_send.at[i - 1], y_recv.at[i - 1], ys_send.at[i - 1], ys_recv.at[i - 1], row(i))
-        copy.start()
-        y_copies.append(copy)
-    gp_own = gp_part(b)
-    z_own[...] = gp_own
+    y_copies = [
+        remote(y_send.at[i], y_recv.at[i], ys_send.at[i], ys_recv.at[i], row(i + 1)) for i in range(batches - 1)
+    ]
+    for at, owner in enumerate((x, left, right, across)):
+        turned[at].wait_recv()
+        here = pl.ds(pl.multiple_of(owner * width, width), width)
+        part = dot(inp_t[here, :], adj_cat[...], 1, 0)
+        offset = (owner + batches - b) % batches
+
+        @pl.when(offset == 0)
+        def _():
+            z_own[...] = part
+
+        @pl.when(offset != 0)
+        def _():
+            to = jnp.maximum(offset - 1, 0)
+            y_send[to] = part.astype(BF16)
+            remote(
+                y_send.at[to], y_recv.at[to], ys_send.at[to], ys_recv.at[to], row(offset)
+            ).start()
 
     def gi_part(owner):
         return dot(adj_bf[...], w_in[pl.ds(pl.multiple_of(owner * width, width), width), :], 1, 1)
@@ -502,7 +508,41 @@
         total += z_recv[j].astype(F32)
     scale = 1.0 / math.sqrt(batches * seqs * steps)
     gp_bf[c, z] = (total * scale).astype(BF16)
-    z_start(lambda i: gp_bf.at[c, z], gp_bf.at[c, z], SPREAD)
+
+    mine = gp_bf.at[c, z]
+
+    def spread(offset, kind, core=c):
+        remote(mine, mine, zs_send.at[kind], zs_recv.at[kind], chip(offset, core)).start()
+
+    def hand(offset, kind):
+        there = gp_bf.at[c, (z + offset) % chips]
+        remote(there, there, pair_send.at[kind], pair_recv.at[kind], partner).start()
+
+    reach = chips // 2
+    near = [sign * d for d in range(min(4, reach - 1), 0, -1) for sign in (1, -1)]
+    far = [sign * d for d in range(reach - 1, 4, -1) for sign in (1, -1)]
+
+    def groups(kind, pair_kind, count, extra):
+        if count == 0 and extra == 0:
+            return (None, None)
+        part = gp_bf.at[c, pl.ds(0, max(count, 1))]
+        more = gp_bf.at[c, pl.ds(0, count + extra)]
+        return (
+            remote(part, part, zs_send.at[kind], zs_recv.at[kind], partner) if count else None,
+            remote(more, more, pair_send.at[pair_kind], pair_recv.at[pair_kind], partner),
+        )
+
+    spread(reach, OPPOSITE, 0)
+    spread(reach, OPPOSITE, 1)
+    for offset in far:
+        spread(offset + chips, FAR)
+    for offset in near:
+        spread(offset + chips, NEAR)
+    hand(0, PAIR_NEAR)
+    near_all, near_hand = groups(NEAR, PAIR_NEAR, len(near), 1)
+    far_all, far_hand = groups(FAR, PAIR_FAR, len(far), 0)
+    two = gp_bf.at[c, pl.ds(0, 2)]
+    opposite_all = remote(two, two, zs_send.at[OPPOSITE], zs_recv.at[OPPOSITE], partner)
 
     own_gi = gi_part(x)
     for i in range(blocks - 1):
@@ -511,6 +551,10 @@
     gi_bf[...] = own_gi.astype(BF16)
     gi_out = local(gi_bf, gi_ref.at[0], 6)
 
+    if near:
+        near_all.wait_recv()
+        for offset in near:
+            hand(offset + chips, PAIR_NEAR)
     for copy in dec_copies:
         copy.wait_recv()
     part = y_dec[0]
@@ -523,19 +567,36 @@
     gd_own[...] = (pair_dec[0] + pair_dec[1]) / (batches * seqs * steps)
     gd_out = local(gd_own, gd_ref, 13)
 
-    z_all(gp_bf.at[c], SPREAD).wait_recv()
-    gp_pair = remote(gp_bf.at[c], gp_bf.at[c], pair_send.at[PAIR_PROJ], pair_recv.at[PAIR_PROJ], partner)
-    gp_pair.start()
-    gp_pair.wait_recv()
-    gp_out = local(gp_bf, gp_ref, 7)
+    if far:
+        far_all.wait_recv()
+        for offset in far:
+            hand(offset + chips, PAIR_FAR)
+    opposite_all.wait_recv()
+    gp_f32[c] = gp_bf[c].astype(F32)
+    gp_outs = [local(gp_f32.at[c], gp_ref.at[c], 7)]
+    near_hand.wait_recv()
+    if far:
+        far_hand.wait_recv()
+    gp_f32[1 - c] = gp_bf[1 - c].astype(F32)
+    gp_outs.append(local(gp_f32.at[1 - c], gp_ref.at[1 - c], 14))
 
     for copy in cot_ring + cot_on + inp_ring + inp_on + turned + gi_copies + y_copies + dec_copies:
         copy.wait_send()
-    for copy in (sum_all, adj_pair, dec_pair, gp_pair):
-        copy.wait_send()
-    for buffer, kind in ((z_dec, DECAY), (z_send, REDUCE), (gp_bf.at[c], SPREAD)):
+    for copy in (sum_all, adj_pair, dec_pair, near_all, near_hand, far_all, far_hand, opposite_all):
+        if copy is not None:
+            copy.wait_send()
+    for buffer, kind in ((z_dec, DECAY), (z_send, REDUCE)):
         z_all(buffer, kind).wait_send()
-    for copy in (gi_out, gp_out, gd_out):
+    for copy in (gi_out, gd_out, *gp_outs):
+        copy.wait()
+
+
+def hand_out(gi_in, gp_in, gd_in, gi_out, gp_out, gd_out, sems):
+    pairs = ((gp_in, gp_out), (gi_in, gi_out), (gd_in, gd_out))
+    copies = [pltpu.make_async_copy(src, dst, sems.at[i]) for i, (src, dst) in enumerate(pairs)]
+    for copy in copies:
+        copy.start()
+    for copy in copies:
         copy.wait()
 
 
@@ -553,7 +614,7 @@
         functools.partial(kernel, sizes),
         out_shape=(
             jax.ShapeDtypeStruct((1, steps, width), BF16),
-            jax.ShapeDtypeStruct((2, chips, piece, states), BF16),
+            jax.ShapeDtypeStruct((2, chips, piece, states), F32),
             jax.ShapeDtypeStruct((2, states), F32),
         ),
         in_specs=[hbm_spec] * 9,
@@ -578,6 +639,7 @@
             pltpu.VMEM((chips, piece, states), BF16),
             pltpu.VMEM((chips, piece, states), BF16),
             pltpu.VMEM((2, chips, piece, states), BF16),
+            pltpu.VMEM((2, chips, piece, states), F32),
             pltpu.VMEM((chips, 2, states), F32),
             pltpu.VMEM((batches, 2, states), F32),
             pltpu.VMEM((2, 2, states), F32),
@@ -588,13 +650,13 @@
             pltpu.SMEM(saved_index.shape, jnp.int32),
             pltpu.VMEM((2, states), F32),
             pltpu.SemaphoreType.REGULAR((4,)),
-            dma((14,)),
+            dma((15,)),
             dma((2, 6)),
             dma((2, 6)),
             dma((PAIR_INPUTS + blocks,)),
             dma((PAIR_INPUTS + blocks,)),
-            dma((4,)),
-            dma((4,)),
+            dma((6,)),
+            dma((6,)),
             dma((batches - 1,)),
             dma((batches - 1,)),
             dma((batches - 1,)),
@@ -606,7 +668,15 @@
             collective_id=0, has_side_effects=True, vmem_limit_bytes=60 * 1024 * 1024
         ),
     )(cotangent, inputs, step_size, resets, log_decay, in_proj, out_proj, saved_states, saved_index)
-    return (grad_inputs, grad_proj.reshape(2, rows, states).astype(F32), grad_decay)
+    results = (grad_inputs, grad_proj.reshape(2, rows, states), grad_decay)
+    return pl.pallas_call(
+        hand_out,
+        out_shape=[jax.ShapeDtypeStruct(part.shape, part.dtype) for part in results],
+        in_specs=[hbm_spec] * 3,
+        out_specs=[hbm_spec] * 3,
+        scratch_shapes=[dma((3,))],
+        compiler_params=pltpu.CompilerParams(vmem_limit_bytes=60 * 1024 * 1024),
+    )(*results)
 
 
 def solution(mesh):

time: 68.4 us -> 90.1 us (1.32)
  Pallas kernels: 64.5 us -> 89.3 us
  other arithmetic: 1.82 us -> 0 us
  local copies, waits for them, and re-layouts: 1.27 us -> 0 us
    pallas_call x0 -> x1, Pallas kernels: none -> 25 us  [local(): pl.pallas_call(hand_out, out_shape=[jax.ShapeDtypeStruct(part.shape, part...]
    convert_element_type x1 -> x0, other arithmetic: 1.82 us -> none  [local(): grad_proj.reshape(2, rows, states).astype(F32)]
    unnamed x6 -> x0, local copies, waits for them, and re-layouts: 1.27 us -> none
where the time goes in v3:
time: 90.1 us; the launch traced here: 90 us
  Pallas kernels  89.3 us (99%)
    pallas_call x1, Pallas kernels, local(): pl.pallas_call(functools.partial(kernel, sizes), out_shape=(jax.ShapeDtyp...  64.3 us
    pallas_call x1, Pallas kernels, local(): pl.pallas_call(hand_out, out_shape=[jax.ShapeDtypeStruct(part.shape, part...  25 us

profile of v3, /device:TPU:1, one launch (start us, length us, event | category | flops | bytes accessed | tf_op | source)
XLA Modules:
  0.0 90.0 jit_solution(9223133092385539902)
XLA Ops:
  0.6 64.3 %shard_map.112 = (bf16[1,256,512]{2,1,0:T(8,128)(2,1)}, f32[2,16,32,128]{3,2,1,0:T(8,128)}, f32[2,128]{1,0:T(2,128)}) custom-call(bf16[1,256,512]{2,1,0:T(8,128)(2,1)} %cot_ref.1, bf16[1,256,512]{2,1,0:T(8,128)(2,1)} %inp_ref.1, f32[1,256]{1,0:T(1,128)} %step_hbm.1, s32[1,256]{1,0:T(1,128)} %resets_hbm.1, f32[2,128]{1,0:T(2,128)} %rate_hbm.1, ...), custom_call_target="tpu_custom_call" | custom-call | tf_op jit(solution)/shard_map/pallas_call | solution.py:613
  65.0 25.0 %shard_map.113 = (bf16[1,256,512]{2,1,0:T(8,128)(2,1)}, f32[2,512,128]{2,1,0:T(8,128)}, f32[2,128]{1,0:T(2,128)}) custom-call(bf16[1,256,512]{2,1,0:T(8,128)(2,1)} %get-tuple-element.6.gi_in, f32[2,512,128]{2,1,0:T(8,128)} %bitcast.1, f32[2,128]{1,0:T(2,128)} %get-tuple-element.8.gd_in), custom_call_target="tpu_custom_call" | custom-call | tf_op jit(solution)/shard_map/pallas_call | solution.py:672

commit v4 on v3

--- a/solution.py
+++ b/solution.py
@@ -591,12 +591,16 @@
         copy.wait()
 
 
-def hand_out(gi_in, gp_in, gd_in, gi_out, gp_out, gd_out, sems):
-    pairs = ((gp_in, gp_out), (gi_in, gi_out), (gd_in, gd_out))
-    copies = [pltpu.make_async_copy(src, dst, sems.at[i]) for i, (src, dst) in enumerate(pairs)]
-    for copy in copies:
+def hand_out(gi_in, gp_in, gd_in, gi_out, gp_out, gd_out, gi, gp, gd, sems):
+    parts = ((gp_in, gp, gp_out), (gi_in, gi, gi_out), (gd_in, gd, gd_out))
+    come = [pltpu.make_async_copy(src, here, sems.at[0, i]) for i, (src, here, _) in enumerate(parts)]
+    go = [pltpu.make_async_copy(here, dst, sems.at[1, i]) for i, (_, here, dst) in enumerate(parts)]
+    for copy in come:
         copy.start()
-    for copy in copies:
+    for first, then in zip(come, go):
+        first.wait()
+        then.start()
+    for copy in go:
         copy.wait()
 
 
@@ -674,7 +678,7 @@
         out_shape=[jax.ShapeDtypeStruct(part.shape, part.dtype) for part in results],
         in_specs=[hbm_spec] * 3,
         out_specs=[hbm_spec] * 3,
-        scratch_shapes=[dma((3,))],
+        scratch_shapes=[*(pltpu.VMEM(part.shape, part.dtype) for part in results), dma((2, 3))],
         compiler_params=pltpu.CompilerParams(vmem_limit_bytes=60 * 1024 * 1024),
     )(*results)
 

time: 90.1 us -> 67.1 us (0.74)
  Pallas kernels: 89.3 us -> 66.3 us
    pallas_call x1, Pallas kernels: 25 us -> 1.97 us  [local(): pl.pallas_call(hand_out, out_shape=[jax.ShapeDtypeStruct(part.shape, part...]
where the time goes in v4:
time: 67.1 us; the launch traced here: 66.9 us
  Pallas kernels  66.3 us (99%)
    pallas_call x1, Pallas kernels, local(): pl.pallas_call(functools.partial(kernel, sizes), out_shape=(jax.ShapeDtyp...  64.3 us
    pallas_call x1, Pallas kernels, local(): pl.pallas_call(hand_out, out_shape=[jax.ShapeDtypeStruct(part.shape, part...  1.97 us

profile of v4, /device:TPU:1, one launch (start us, length us, event | category | flops | bytes accessed | tf_op | source)
XLA Modules:
  0.0 66.9 jit_solution(6869649627383189858)
XLA Ops:
  0.6 64.3 %shard_map.112 = (bf16[1,256,512]{2,1,0:T(8,128)(2,1)}, f32[2,16,32,128]{3,2,1,0:T(8,128)}, f32[2,128]{1,0:T(2,128)}) custom-call(bf16[1,256,512]{2,1,0:T(8,128)(2,1)} %cot_ref.1, bf16[1,256,512]{2,1,0:T(8,128)(2,1)} %inp_ref.1, f32[1,256]{1,0:T(1,128)} %step_hbm.1, s32[1,256]{1,0:T(1,128)} %resets_hbm.1, f32[2,128]{1,0:T(2,128)} %rate_hbm.1, ...), custom_call_target="tpu_custom_call" | custom-call | tf_op jit(solution)/shard_map/pallas_call | solution.py:617
  65.0 2.0 %shard_map.113 = (bf16[1,256,512]{2,1,0:T(8,128)(2,1)}, f32[2,512,128]{2,1,0:T(8,128)}, f32[2,128]{1,0:T(2,128)}) custom-call(bf16[1,256,512]{2,1,0:T(8,128)(2,1)} %get-tuple-element.6.gi_in, f32[2,512,128]{2,1,0:T(8,128)} %bitcast.1, f32[2,128]{1,0:T(2,128)} %get-tuple-element.8.gd_in), custom_call_target="tpu_custom_call" | custom-call | tf_op jit(solution)/shard_map/pallas_call | solution.py:676

commit v5 on v4

--- a/solution.py
+++ b/solution.py
@@ -12,8 +12,10 @@
 F32 = jnp.float32
 BF16 = jnp.bfloat16
 GROUPS = 8
-SUMMARY, DECAY, REDUCE, NEAR, FAR, OPPOSITE = range(6)
-PAIR_ADJOINT, PAIR_DECAY, PAIR_NEAR, PAIR_FAR, PAIR_INPUTS = range(5)
+CLASSES = 4
+SUMMARY, DECAY = range(2)
+PAIR_ADJOINT, PAIR_DECAY, PAIR_PROJ = range(3)
+PAIR_INPUTS = PAIR_PROJ + 3
 
 
 def complex_times(left_re, left_im, right_re, right_im):
@@ -109,11 +111,11 @@
     gi_send,
     gi_recv,
     gi_bf,
-    y_send,
-    y_recv,
+    g_send,
+    g_full,
+    g_half,
     z_own,
-    z_send,
-    z_recv,
+    z_mem,
     gp_bf,
     gp_f32,
     z_dec,
@@ -133,8 +135,12 @@
     pair_recv,
     zs_send,
     zs_recv,
-    ys_send,
-    ys_recv,
+    gs_send,
+    gs_recv,
+    zm_send,
+    zm_recv,
+    sp_send,
+    sp_recv,
     yd_send,
     yd_recv,
     gi_ssem,
@@ -146,8 +152,7 @@
     half = steps // 2
     length = steps // GROUPS
     states = dec_re.shape[1]
-    rows = y_recv.shape[1]
-    piece = z_recv.shape[1]
+    piece = z_mem.shape[1]
     s, b, x = lax.axis_index("seq"), lax.axis_index("batch"), lax.axis_index("state")
     z, c = s // 2, s % 2
     partner = {"seq": 2 * z + (1 - c)}
@@ -266,6 +271,7 @@
     inject += part_dot(cot_all, w_out, right)
     round_end(2)
     greet(known_sem.at[3], [partner])
+    greet(known_sem.at[4], [row(i) for i in range(1, batches)])
     for copy in cot_on:
         copy.wait_recv()
     inject += part_dot(cot_all, w_out, across)
@@ -402,14 +408,30 @@
     turned.append(turn(across, 3))
 
     adj_pair.wait_recv()
-    y_copies = [
-        remote(y_send.at[i], y_recv.at[i], ys_send.at[i], ys_recv.at[i], row(i + 1)) for i in range(batches - 1)
-    ]
+    pl.semaphore_wait(known_sem.at[4], batches - 1)
+    kind = z % CLASSES
+    around = (2, -2, 1, -1, 0)
+
+    def class_rows(of, at):
+        start = of * piece + (piece // 2 if at == -2 else 0)
+        size = piece // 2 if abs(at) == 2 else piece
+        return pl.ds(pl.multiple_of(start, size), size)
+
+    def near_copy(offset, at):
+        src = g_send.at[offset, class_rows((z + at + chips) % CLASSES, at)]
+        place = around.index(at)
+        dst = g_half.at[offset, place] if abs(at) == 2 else g_full.at[offset, place - 2]
+        device = {"seq": 2 * ((z + at + chips) % chips) + c, "batch": (b + offset) % batches}
+        return remote(src, dst, gs_send.at[offset, place], gs_recv.at[offset, place], device)
+
     for at, owner in enumerate((x, left, right, across)):
         turned[at].wait_recv()
         here = pl.ds(pl.multiple_of(owner * width, width), width)
         part = dot(inp_t[here, :], adj_cat[...], 1, 0)
         offset = (owner + batches - b) % batches
+        g_send[offset] = part.astype(BF16)
+        for distance in around[:-1]:
+            near_copy(offset, distance).start()
 
         @pl.when(offset == 0)
         def _():
@@ -417,11 +439,14 @@
 
         @pl.when(offset != 0)
         def _():
-            to = jnp.maximum(offset - 1, 0)
-            y_send[to] = part.astype(BF16)
-            remote(
-                y_send.at[to], y_recv.at[to], ys_send.at[to], ys_recv.at[to], row(offset)
-            ).start()
+            near_copy(offset, 0).start()
+
+    g_copies = {
+        (offset, distance): near_copy(offset, distance)
+        for offset in range(batches)
+        for distance in around
+        if offset or distance
+    }
 
     def gi_part(owner):
         return dot(adj_bf[...], w_in[pl.ds(pl.multiple_of(owner * width, width), width), :], 1, 1)
@@ -481,15 +506,21 @@
     )
     z_start(lambda i: z_dec.at[z], z_dec.at[z], DECAY)
 
-    for copy in y_copies:
+    for copy in g_copies.values():
         copy.wait_recv()
-    total = z_own[...]
-    for i in range(batches - 1):
-        total += y_recv[i].astype(F32)
-    z_own[...] = total
-    z_send[...] = total.reshape(chips, piece, states).astype(BF16)
-    z_recv[z] = jnp.zeros((piece, states), BF16)
-    z_start(lambda i: z_send.at[(z + i) % chips], z_recv.at[z], REDUCE)
+    total = z_own[class_rows(kind, 0), :]
+    for offset in range(batches):
+        if offset:
+            total += g_full[offset, 2].astype(F32)
+        total += g_full[offset, 0].astype(F32) + g_full[offset, 1].astype(F32)
+        total += jnp.concatenate([g_half[offset, 0], g_half[offset, 1]], axis=0).astype(F32)
+    z_mem[z // CLASSES] = total.astype(BF16)
+    member = z_mem.at[z // CLASSES]
+    members = []
+    for i in range(chips // CLASSES - 1):
+        copy = remote(member, member, zm_send.at[i], zm_recv.at[i], chip(CLASSES * (i + 1)))
+        copy.start()
+        members.append(copy)
 
     z_all(z_dec, DECAY).wait_recv()
     part = z_dec[0]
@@ -502,47 +533,30 @@
         copy.start()
         dec_copies.append(copy)
 
-    z_all(z_recv, REDUCE).wait_recv()
-    total = z_own[pl.ds(pl.multiple_of(z * piece, piece), piece), :]
-    for j in range(chips):
-        total += z_recv[j].astype(F32)
+    for copy in members:
+        copy.wait_recv()
+    total = z_mem[0].astype(F32)
+    for i in range(1, chips // CLASSES):
+        total += z_mem[i].astype(F32)
     scale = 1.0 / math.sqrt(batches * seqs * steps)
-    gp_bf[c, z] = (total * scale).astype(BF16)
-
-    mine = gp_bf.at[c, z]
-
-    def spread(offset, kind, core=c):
-        remote(mine, mine, zs_send.at[kind], zs_recv.at[kind], chip(offset, core)).start()
-
-    def hand(offset, kind):
-        there = gp_bf.at[c, (z + offset) % chips]
-        remote(there, there, pair_send.at[kind], pair_recv.at[kind], partner).start()
-
-    reach = chips // 2
-    near = [sign * d for d in range(min(4, reach - 1), 0, -1) for sign in (1, -1)]
-    far = [sign * d for d in range(reach - 1, 4, -1) for sign in (1, -1)]
-
-    def groups(kind, pair_kind, count, extra):
-        if count == 0 and extra == 0:
-            return (None, None)
-        part = gp_bf.at[c, pl.ds(0, max(count, 1))]
-        more = gp_bf.at[c, pl.ds(0, count + extra)]
-        return (
-            remote(part, part, zs_send.at[kind], zs_recv.at[kind], partner) if count else None,
-            remote(more, more, pair_send.at[pair_kind], pair_recv.at[pair_kind], partner),
-        )
-
-    spread(reach, OPPOSITE, 0)
-    spread(reach, OPPOSITE, 1)
-    for offset in far:
-        spread(offset + chips, FAR)
-    for offset in near:
-        spread(offset + chips, NEAR)
-    hand(0, PAIR_NEAR)
-    near_all, near_hand = groups(NEAR, PAIR_NEAR, len(near), 1)
-    far_all, far_hand = groups(FAR, PAIR_FAR, len(far), 0)
-    two = gp_bf.at[c, pl.ds(0, 2)]
-    opposite_all = remote(two, two, zs_send.at[OPPOSITE], zs_recv.at[OPPOSITE], partner)
+    gp_bf[c, kind] = (total * scale).astype(BF16)
+
+    def spread(at, core, place):
+        rows_of = pl.ds(piece // 2 if at == -2 else 0, piece // 2 if abs(at) == 2 else piece)
+        mine = gp_bf.at[c, kind, rows_of]
+        copy = remote(mine, mine, sp_send.at[place], sp_recv.at[place], chip(at + chips, core))
+        copy.start()
+        return copy
+
+    def hand(of, place):
+        there = gp_bf.at[c, of]
+        copy = remote(there, there, pair_send.at[place], pair_recv.at[place], partner)
+        copy.start()
+        return copy
+
+    halves = [spread(at, core, place) for place, (at, core) in enumerate(((2, c), (-2, c), (2, 1 - c), (-2, 1 - c)))]
+    wholes = [spread(1, c, 4), spread(-1, c, 5)]
+    hands = [hand(kind, PAIR_PROJ)]
 
     own_gi = gi_part(x)
     for i in range(blocks - 1):
@@ -551,10 +565,10 @@
     gi_bf[...] = own_gi.astype(BF16)
     gi_out = local(gi_bf, gi_ref.at[0], 6)
 
-    if near:
-        near_all.wait_recv()
-        for offset in near:
-            hand(offset + chips, PAIR_NEAR)
+    wholes[0].wait_recv()
+    hands.append(hand((kind + CLASSES - 1) % CLASSES, PAIR_PROJ + 1))
+    wholes[1].wait_recv()
+    hands.append(hand((kind + 1) % CLASSES, PAIR_PROJ + 2))
     for copy in dec_copies:
         copy.wait_recv()
     part = y_dec[0]
@@ -567,26 +581,20 @@
     gd_own[...] = (pair_dec[0] + pair_dec[1]) / (batches * seqs * steps)
     gd_out = local(gd_own, gd_ref, 13)
 
-    if far:
-        far_all.wait_recv()
-        for offset in far:
-            hand(offset + chips, PAIR_FAR)
-    opposite_all.wait_recv()
+    for copy in halves[:2]:
+        copy.wait_recv()
     gp_f32[c] = gp_bf[c].astype(F32)
     gp_outs = [local(gp_f32.at[c], gp_ref.at[c], 7)]
-    near_hand.wait_recv()
-    if far:
-        far_hand.wait_recv()
+    for copy in halves[2:] + hands:
+        copy.wait_recv()
     gp_f32[1 - c] = gp_bf[1 - c].astype(F32)
     gp_outs.append(local(gp_f32.at[1 - c], gp_ref.at[1 - c], 14))
 
-    for copy in cot_ring + cot_on + inp_ring + inp_on + turned + gi_copies + y_copies + dec_copies:
+    for copy in cot_ring + cot_on + inp_ring + inp_on + turned + gi_copies + dec_copies:
         copy.wait_send()
-    for copy in (sum_all, adj_pair, dec_pair, near_all, near_hand, far_all, far_hand, opposite_all):
-        if copy is not None:
-            copy.wait_send()
-    for buffer, kind in ((z_dec, DECAY), (z_send, REDUCE)):
-        z_all(buffer, kind).wait_send()
+    for copy in (sum_all, adj_pair, dec_pair, *g_copies.values(), *members, *halves, *wholes, *hands):
+        copy.wait_send()
+    z_all(z_dec, DECAY).wait_send()
     for copy in (gi_out, gd_out, *gp_outs):
         copy.wait()
 
@@ -610,7 +618,7 @@
     _, steps, width = inputs.shape
     _, features, states = in_proj.shape
     rows = features // batches
-    piece = rows // chips
+    piece = rows // CLASSES
     hbm_spec = pl.BlockSpec(memory_space=pltpu.HBM)
     per_step = pltpu.VMEM((steps, states), F32)
     dma = pltpu.SemaphoreType.DMA
@@ -618,7 +626,7 @@
         functools.partial(kernel, sizes),
         out_shape=(
             jax.ShapeDtypeStruct((1, steps, width), BF16),
-            jax.ShapeDtypeStruct((2, chips, piece, states), F32),
+            jax.ShapeDtypeStruct((2, CLASSES, piece, states), F32),
             jax.ShapeDtypeStruct((2, states), F32),
         ),
         in_specs=[hbm_spec] * 9,
@@ -637,13 +645,13 @@
             pltpu.VMEM((blocks - 1, steps, width), BF16),
             pltpu.VMEM((blocks - 1, steps, width), BF16),
             pltpu.VMEM((steps, width), BF16),
-            pltpu.VMEM((batches - 1, rows, states), BF16),
-            pltpu.VMEM((batches - 1, rows, states), BF16),
+            pltpu.VMEM((batches, rows, states), BF16),
+            pltpu.VMEM((batches, 3, piece, states), BF16),
+            pltpu.VMEM((batches, 2, piece // 2, states), BF16),
             pltpu.VMEM((rows, states), F32),
-            pltpu.VMEM((chips, piece, states), BF16),
-            pltpu.VMEM((chips, piece, states), BF16),
-            pltpu.VMEM((2, chips, piece, states), BF16),
-            pltpu.VMEM((2, chips, piece, states), F32),
+            pltpu.VMEM((chips // CLASSES, piece, states), BF16),
+            pltpu.VMEM((2, CLASSES, piece, states), BF16),
+            pltpu.VMEM((2, CLASSES, piece, states), F32),
             pltpu.VMEM((chips, 2, states), F32),
             pltpu.VMEM((batches, 2, states), F32),
             pltpu.VMEM((2, 2, states), F32),
@@ -653,16 +661,20 @@
             pltpu.VMEM(saved_states.shape, F32),
             pltpu.SMEM(saved_index.shape, jnp.int32),
             pltpu.VMEM((2, states), F32),
-            pltpu.SemaphoreType.REGULAR((4,)),
+            pltpu.SemaphoreType.REGULAR((5,)),
             dma((15,)),
             dma((2, 6)),
             dma((2, 6)),
             dma((PAIR_INPUTS + blocks,)),
             dma((PAIR_INPUTS + blocks,)),
+            dma((2,)),
+            dma((2,)),
+            dma((batches, 5)),
+            dma((batches, 5)),
+            dma((chips // CLASSES,)),
+            dma((chips // CLASSES,)),
             dma((6,)),
             dma((6,)),
-            dma((batches - 1,)),
-            dma((batches - 1,)),
             dma((batches - 1,)),
             dma((batches - 1,)),
             dma((blocks - 1,)),

time: 67.1 us -> 65.6 us (0.978)
  the two profiles are of different devices: /device:TPU:1 before, /device:TPU:15 now
where the time goes in v5:
time: 65.6 us; the launch traced here: 65.4 us
  Pallas kernels  64.8 us (99%)
    pallas_call x1, Pallas kernels, local(): pl.pallas_call(functools.partial(kernel, sizes), out_shape=(jax.ShapeDtyp...  62.8 us
    pallas_call x1, Pallas kernels, local(): pl.pallas_call(hand_out, out_shape=[jax.ShapeDtypeStruct(part.shape, part...  1.97 us

profile of v5, /device:TPU:15, one launch (start us, length us, event | category | flops | bytes accessed | tf_op | source)
XLA Modules:
  0.0 65.4 jit_solution(15907766611277351683)
XLA Ops:
  0.6 62.8 %shard_map.112 = (bf16[1,256,512]{2,1,0:T(8,128)(2,1)}, f32[2,4,128,128]{3,2,1,0:T(8,128)}, f32[2,128]{1,0:T(2,128)}) custom-call(bf16[1,256,512]{2,1,0:T(8,128)(2,1)} %cot_ref.1, bf16[1,256,512]{2,1,0:T(8,128)(2,1)} %inp_ref.1, f32[1,256]{1,0:T(1,128)} %step_hbm.1, s32[1,256]{1,0:T(1,128)} %resets_hbm.1, f32[2,128]{1,0:T(2,128)} %rate_hbm.1, ...), custom_call_target="tpu_custom_call" | custom-call | tf_op jit(solution)/shard_map/pallas_call | solution.py:625
  63.5 2.0 %shard_map.113 = (bf16[1,256,512]{2,1,0:T(8,128)(2,1)}, f32[2,512,128]{2,1,0:T(8,128)}, f32[2,128]{1,0:T(2,128)}) custom-call(bf16[1,256,512]{2,1,0:T(8,128)(2,1)} %get-tuple-element.6.gi_in, f32[2,512,128]{2,1,0:T(8,128)} %bitcast.1, f32[2,128]{1,0:T(2,128)} %get-tuple-element.8.gd_in), custom_call_target="tpu_custom_call" | custom-call | tf_op jit(solution)/shard_map/pallas_call | solution.py:688

commit v6 on v5

--- a/solution.py
+++ b/solution.py
@@ -117,7 +117,6 @@
     z_own,
     z_mem,
     gp_bf,
-    gp_f32,
     z_dec,
     y_dec,
     pair_dec,
@@ -177,7 +176,7 @@
     peers = [partner]
     peers += [block(i) for i in range(1, blocks)]
     peers += [row(i) for i in range(1, batches)]
-    peers += [chip(1), chip(chips - 1)]
+    peers += [chip(offset, core) for offset in (1, chips - 1) for core in (c, 1 - c)]
 
     def greet(semaphore, devices):
         for device in devices:
@@ -189,11 +188,12 @@
 
     def round_start(at):
         if at < len(rounds):
-            greet(known_sem.at[at], [chip(rounds[at]), chip(chips - rounds[at])])
+            both = (rounds[at], chips - rounds[at])
+            greet(known_sem.at[at], [chip(offset, core) for offset in both for core in (c, 1 - c)])
 
     def round_end(at):
         if at < len(rounds):
-            pl.semaphore_wait(known_sem.at[at], 2)
+            pl.semaphore_wait(known_sem.at[at], 4)
 
     def local(src, dst, at):
         copy = pltpu.make_async_copy(src, dst, local_sem.at[at])
@@ -255,23 +255,22 @@
     cot_own.wait()
     for copy in out_copies:
         copy.wait()
-    inject = part_dot(cot_all, w_out, x)
     round_end(0)
     round_start(1)
+    inject = part_dot(cot_all, w_out, x)
     cot_ring[0].wait_recv()
     cot_on = [forward(cot_all, 0, 0)]
     cot_ring[1].wait_recv()
     cot_on.append(forward(cot_all, 0, 1))
-    inp_ring = ring(inp_ref, inp_all, 1)
     round_end(1)
     round_start(2)
+    inp_ring = ring(inp_ref, inp_all, 1)
     cot_ring[2].wait_recv()
     inject += part_dot(cot_all, w_out, left)
     cot_ring[3].wait_recv()
     inject += part_dot(cot_all, w_out, right)
     round_end(2)
-    greet(known_sem.at[3], [partner])
-    greet(known_sem.at[4], [row(i) for i in range(1, batches)])
+    greet(known_sem.at[3], [row(i) for i in range(1, batches)])
     for copy in cot_on:
         copy.wait_recv()
     inject += part_dot(cot_all, w_out, across)
@@ -308,7 +307,6 @@
     for g in range(GROUPS - 2, -1, -1):
         own = compose(own, grp_rows[g])
     z_sum[s] = jnp.concatenate(own, axis=0)
-    pl.semaphore_wait(known_sem.at[3], 1)
 
     def four(ref, at):
         return tuple(ref[at, k : k + 1, :] for k in range(4))
@@ -365,6 +363,10 @@
     inp_ring[3].wait_recv()
     turned.append(turn(right, 2))
     drive += part_dot(inp_all, w_in, right)
+    for copy in inp_on:
+        copy.wait_recv()
+    turned.append(turn(across, 3))
+
     sum_all.wait_recv()
     in_re, in_im = jnp.zeros((1, states), F32), jnp.zeros((1, states), F32)
     for j in range(seqs - 1, 0, -1):
@@ -403,12 +405,9 @@
         adj_send, adj_cat.at[own_rows], pair_send.at[PAIR_ADJOINT], pair_recv.at[PAIR_ADJOINT], partner
     )
     adj_pair.start()
-    for copy in inp_on:
-        copy.wait_recv()
-    turned.append(turn(across, 3))
 
     adj_pair.wait_recv()
-    pl.semaphore_wait(known_sem.at[4], batches - 1)
+    pl.semaphore_wait(known_sem.at[3], batches - 1)
     kind = z % CLASSES
     around = (2, -2, 1, -1, 0)
 
@@ -424,21 +423,19 @@
         device = {"seq": 2 * ((z + at + chips) % chips) + c, "batch": (b + offset) % batches}
         return remote(src, dst, gs_send.at[offset, place], gs_recv.at[offset, place], device)
 
-    for at, owner in enumerate((x, left, right, across)):
-        turned[at].wait_recv()
+    for copy in turned:
+        copy.wait_recv()
+    for place, offset in enumerate((2, 1, 3, 0)):
+        owner = (b + offset) % batches
         here = pl.ds(pl.multiple_of(owner * width, width), width)
         part = dot(inp_t[here, :], adj_cat[...], 1, 0)
-        offset = (owner + batches - b) % batches
         g_send[offset] = part.astype(BF16)
         for distance in around[:-1]:
             near_copy(offset, distance).start()
 
-        @pl.when(offset == 0)
-        def _():
+        if place == 3:
             z_own[...] = part
-
-        @pl.when(offset != 0)
-        def _():
+        else:
             near_copy(offset, 0).start()
 
     g_copies = {
@@ -583,12 +580,10 @@
 
     for copy in halves[:2]:
         copy.wait_recv()
-    gp_f32[c] = gp_bf[c].astype(F32)
-    gp_outs = [local(gp_f32.at[c], gp_ref.at[c], 7)]
+    gp_outs = [local(gp_bf.at[c], gp_ref.at[c], 7)]
     for copy in halves[2:] + hands:
         copy.wait_recv()
-    gp_f32[1 - c] = gp_bf[1 - c].astype(F32)
-    gp_outs.append(local(gp_f32.at[1 - c], gp_ref.at[1 - c], 14))
+    gp_outs.append(local(gp_bf.at[1 - c], gp_ref.at[1 - c], 14))
 
     for copy in cot_ring + cot_on + inp_ring + inp_on + turned + gi_copies + dec_copies:
         copy.wait_send()
@@ -599,15 +594,18 @@
         copy.wait()
 
 
-def hand_out(gi_in, gp_in, gd_in, gi_out, gp_out, gd_out, gi, gp, gd, sems):
-    parts = ((gp_in, gp, gp_out), (gi_in, gi, gi_out), (gd_in, gd, gd_out))
-    come = [pltpu.make_async_copy(src, here, sems.at[0, i]) for i, (src, here, _) in enumerate(parts)]
-    go = [pltpu.make_async_copy(here, dst, sems.at[1, i]) for i, (_, here, dst) in enumerate(parts)]
+def hand_out(gi_in, gp_in, gd_in, gi_out, gp_out, gd_out, gi, gp, gd, wide, sems):
+    parts = [(gp_in.at[k], gp.at[k], wide.at[k], gp_out.at[k]) for k in range(2)]
+    parts += [(gi_in, gi, gi, gi_out), (gd_in, gd, gd, gd_out)]
+    come = [pltpu.make_async_copy(part[0], part[1], sems.at[0, i]) for i, part in enumerate(parts)]
+    go = [pltpu.make_async_copy(part[2], part[3], sems.at[1, i]) for i, part in enumerate(parts)]
     for copy in come:
         copy.start()
-    for first, then in zip(come, go):
-        first.wait()
-        then.start()
+    for i in range(len(parts)):
+        come[i].wait()
+        if i < 2:
+            wide[i] = gp[i].astype(F32)
+        go[i].start()
     for copy in go:
         copy.wait()
 
@@ -626,7 +624,7 @@
         functools.partial(kernel, sizes),
         out_shape=(
             jax.ShapeDtypeStruct((1, steps, width), BF16),
-            jax.ShapeDtypeStruct((2, CLASSES, piece, states), F32),
+            jax.ShapeDtypeStruct((2, CLASSES, piece, states), BF16),
             jax.ShapeDtypeStruct((2, states), F32),
         ),
         in_specs=[hbm_spec] * 9,
@@ -651,7 +649,6 @@
             pltpu.VMEM((rows, states), F32),
             pltpu.VMEM((chips // CLASSES, piece, states), BF16),
             pltpu.VMEM((2, CLASSES, piece, states), BF16),
-            pltpu.VMEM((2, CLASSES, piece, states), F32),
             pltpu.VMEM((chips, 2, states), F32),
             pltpu.VMEM((batches, 2, states), F32),
             pltpu.VMEM((2, 2, states), F32),
@@ -661,7 +658,7 @@
             pltpu.VMEM(saved_states.shape, F32),
             pltpu.SMEM(saved_index.shape, jnp.int32),
             pltpu.VMEM((2, states), F32),
-            pltpu.SemaphoreType.REGULAR((5,)),
+            pltpu.SemaphoreType.REGULAR((4,)),
             dma((15,)),
             dma((2, 6)),
             dma((2, 6)),
@@ -687,10 +684,18 @@
     results = (grad_inputs, grad_proj.reshape(2, rows, states), grad_decay)
     return pl.pallas_call(
         hand_out,
-        out_shape=[jax.ShapeDtypeStruct(part.shape, part.dtype) for part in results],
+        out_shape=[
+            jax.ShapeDtypeStruct(grad_inputs.shape, BF16),
+            jax.ShapeDtypeStruct((2, rows, states), F32),
+            jax.ShapeDtypeStruct(grad_decay.shape, F32),
+        ],
         in_specs=[hbm_spec] * 3,
         out_specs=[hbm_spec] * 3,
-        scratch_shapes=[*(pltpu.VMEM(part.shape, part.dtype) for part in results), dma((2, 3))],
+        scratch_shapes=[
+            *(pltpu.VMEM(part.shape, part.dtype) for part in results),
+            pltpu.VMEM((2, rows, states), F32),
+            dma((2, 4)),
+        ],
         compiler_params=pltpu.CompilerParams(vmem_limit_bytes=60 * 1024 * 1024),
     )(*results)
 

time: 65.6 us -> 63.9 us (0.974)
  the two profiles are of different devices: /device:TPU:15 before, /device:TPU:1 now
where the time goes in v6:
time: 63.9 us; the launch traced here: 63.8 us
  Pallas kernels  63.1 us (99%)
  between operations  0.64 us (1%)
    pallas_call x1, Pallas kernels, local(): pl.pallas_call(functools.partial(kernel, sizes), out_shape=(jax.ShapeDtyp...  61.2 us
    pallas_call x1, Pallas kernels, local(): pl.pallas_call(hand_out, out_shape=[jax.ShapeDtypeStruct(grad_inputs.shap...  1.87 us

profile of v6, /device:TPU:1, one launch (start us, length us, event | category | flops | bytes accessed | tf_op | source)
XLA Modules:
  0.0 63.8 jit_solution(520493522762559051)
XLA Ops:
  0.6 61.2 %shard_map.112 = (bf16[1,256,512]{2,1,0:T(8,128)(2,1)}, bf16[2,4,128,128]{3,2,1,0:T(8,128)(2,1)}, f32[2,128]{1,0:T(2,128)}) custom-call(bf16[1,256,512]{2,1,0:T(8,128)(2,1)} %cot_ref.1, bf16[1,256,512]{2,1,0:T(8,128)(2,1)} %inp_ref.1, f32[1,256]{1,0:T(1,128)} %step_hbm.1, s32[1,256]{1,0:T(1,128)} %resets_hbm.1, f32[2,128]{1,0:T(2,128)} %rate_hbm.1, ...), custom_call_target="tpu_custom_call" | custom-call | tf_op jit(solution)/shard_map/pallas_call | solution.py:623
  61.9 1.9 %shard_map.113 = (bf16[1,256,512]{2,1,0:T(8,128)(2,1)}, f32[2,512,128]{2,1,0:T(8,128)}, f32[2,128]{1,0:T(2,128)}) custom-call(bf16[1,256,512]{2,1,0:T(8,128)(2,1)} %get-tuple-element.6.gi_in, bf16[2,512,128]{2,1,0:T(8,128)(2,1)} %bitcast.1, f32[2,128]{1,0:T(2,128)} %get-tuple-element.8.gd_in), custom_call_target="tpu_custom_call" | custom-call | tf_op jit(solution)/shard_map/pallas_call | solution.py:685

commit v7 on v6

--- a/solution.py
+++ b/solution.py
@@ -202,12 +202,6 @@
 
     cot_own = local(cot_ref.at[0], cot_all.at[x], 0)
     out_copies = [local(w_out_ref.at[k], w_out.at[:, pl.ds(k * states, states)], 1 + k) for k in range(2)]
-    inp_own = local(inp_ref.at[0], inp_all.at[x], 3)
-    small = ((step_hbm, step_ref), (resets_hbm, resets_ref), (rate_hbm, rate_ref))
-    small_copies = [local(*pair, 8 + k) for k, pair in enumerate(small)]
-    saved_copies = [local(saved_hbm, saved_ref, 11), local(index_hbm, index_ref, 12)]
-    in_copies = [local(w_in_ref.at[k], w_in.at[:, pl.ds(k * states, states)], 4 + k) for k in range(2)]
-
     pl.semaphore_wait(barrier, len(peers))
     round_start(0)
 
@@ -237,6 +231,11 @@
         return copy
 
     cot_ring = ring(cot_ref, cot_all, 0)
+    inp_own = local(inp_ref.at[0], inp_all.at[x], 3)
+    small = ((step_hbm, step_ref), (resets_hbm, resets_ref), (rate_hbm, rate_ref))
+    small_copies = [local(*pair, 8 + k) for k, pair in enumerate(small)]
+    saved_copies = [local(saved_hbm, saved_ref, 11), local(index_hbm, index_ref, 12)]
+    in_copies = [local(w_in_ref.at[k], w_in.at[:, pl.ds(k * states, states)], 4 + k) for k in range(2)]
 
     for copy in small_copies:
         copy.wait()
@@ -395,8 +394,6 @@
         unroll=True,
     )
     bf_re, bf_im = adj_re[...].astype(BF16), adj_im[...].astype(BF16)
-    adj_bf[:, :states] = bf_re
-    adj_bf[:, states:] = bf_im
     first = (jnp.zeros((steps, states), jnp.int32) + c) == 0
     own_rows = pl.ds(pl.multiple_of(c * steps, steps), steps)
     adj_send[...] = jnp.where(first, adj_im[...], adj_re[...]).astype(BF16)
@@ -405,6 +402,8 @@
         adj_send, adj_cat.at[own_rows], pair_send.at[PAIR_ADJOINT], pair_recv.at[PAIR_ADJOINT], partner
     )
     adj_pair.start()
+    adj_bf[:, :states] = bf_re
+    adj_bf[:, states:] = bf_im
 
     adj_pair.wait_recv()
     pl.semaphore_wait(known_sem.at[3], batches - 1)
@@ -540,19 +539,21 @@
 
     def spread(at, core, place):
         rows_of = pl.ds(piece // 2 if at == -2 else 0, piece // 2 if abs(at) == 2 else piece)
-        mine = gp_bf.at[c, kind, rows_of]
-        copy = remote(mine, mine, sp_send.at[place], sp_recv.at[place], chip(at + chips, core))
+        there = gp_ref if abs(at) == 2 else gp_bf
+        mine, target = gp_bf.at[c, kind, rows_of], there.at[c, kind, rows_of]
+        copy = remote(mine, target, sp_send.at[place], sp_recv.at[place], chip(at + chips, core))
         copy.start()
         return copy
 
     def hand(of, place):
-        there = gp_bf.at[c, of]
-        copy = remote(there, there, pair_send.at[place], pair_recv.at[place], partner)
+        gp_outs.append(local(gp_bf.at[c, of], gp_ref.at[c, of], 15 + place - PAIR_PROJ))
+        copy = remote(gp_bf.at[c, of], gp_ref.at[c, of], pair_send.at[place], pair_recv.at[place], partner)
         copy.start()
         return copy
 
+    gp_outs = []
+    wholes = [spread(1, c, 4), spread(-1, c, 5)]
     halves = [spread(at, core, place) for place, (at, core) in enumerate(((2, c), (-2, c), (2, 1 - c), (-2, 1 - c)))]
-    wholes = [spread(1, c, 4), spread(-1, c, 5)]
     hands = [hand(kind, PAIR_PROJ)]
 
     own_gi = gi_part(x)
@@ -578,12 +579,8 @@
     gd_own[...] = (pair_dec[0] + pair_dec[1]) / (batches * seqs * steps)
     gd_out = local(gd_own, gd_ref, 13)
 
-    for copy in halves[:2]:
+    for copy in halves + hands:
         copy.wait_recv()
-    gp_outs = [local(gp_bf.at[c], gp_ref.at[c], 7)]
-    for copy in halves[2:] + hands:
-        copy.wait_recv()
-    gp_outs.append(local(gp_bf.at[1 - c], gp_ref.at[1 - c], 14))
 
     for copy in cot_ring + cot_on + inp_ring + inp_on + turned + gi_copies + dec_copies:
         copy.wait_send()
@@ -659,7 +656,7 @@
             pltpu.SMEM(saved_index.shape, jnp.int32),
             pltpu.VMEM((2, states), F32),
             pltpu.SemaphoreType.REGULAR((4,)),
-            dma((15,)),
+            dma((18,)),
             dma((2, 6)),
             dma((2, 6)),
             dma((PAIR_INPUTS + blocks,)),

time: 63.9 us -> 63.2 us (0.989)
  Pallas kernels: 63.1 us -> 62.4 us
    pallas_call x1, Pallas kernels: 61.2 us -> 60.5 us  [local(): pl.pallas_call(functools.partial(kernel, sizes), out_shape=(jax.ShapeDtyp...]
where the time goes in v7:
time: 63.2 us; the launch traced here: 63 us
  Pallas kernels  62.4 us (99%)
  between operations  0.64 us (1%)
    pallas_call x1, Pallas kernels, local(): pl.pallas_call(functools.partial(kernel, sizes), out_shape=(jax.ShapeDtyp...  60.5 us
    pallas_call x1, Pallas kernels, local(): pl.pallas_call(hand_out, out_shape=[jax.ShapeDtypeStruct(grad_inputs.shap...  1.87 us

profile of v7, /device:TPU:1, one launch (start us, length us, event | category | flops | bytes accessed | tf_op | source)
XLA Modules:
  0.0 63.0 jit_solution(15764128277014487086)
XLA Ops:
  0.6 60.5 %shard_map.112 = (bf16[1,256,512]{2,1,0:T(8,128)(2,1)}, bf16[2,4,128,128]{3,2,1,0:T(8,128)(2,1)}, f32[2,128]{1,0:T(2,128)}) custom-call(bf16[1,256,512]{2,1,0:T(8,128)(2,1)} %cot_ref.1, bf16[1,256,512]{2,1,0:T(8,128)(2,1)} %inp_ref.1, f32[1,256]{1,0:T(1,128)} %step_hbm.1, s32[1,256]{1,0:T(1,128)} %resets_hbm.1, f32[2,128]{1,0:T(2,128)} %rate_hbm.1, ...), custom_call_target="tpu_custom_call" | custom-call | tf_op jit(solution)/shard_map/pallas_call | solution.py:620
  61.2 1.9 %shard_map.113 = (bf16[1,256,512]{2,1,0:T(8,128)(2,1)}, f32[2,512,128]{2,1,0:T(8,128)}, f32[2,128]{1,0:T(2,128)}) custom-call(bf16[1,256,512]{2,1,0:T(8,128)(2,1)} %get-tuple-element.6.gi_in, bf16[2,512,128]{2,1,0:T(8,128)(2,1)} %bitcast.1, f32[2,128]{1,0:T(2,128)} %get-tuple-element.8.gd_in), custom_call_target="tpu_custom_call" | custom-call | tf_op jit(solution)/shard_map/pallas_call | solution.py:682

commit v8 on v7

--- a/solution.py
+++ b/solution.py
@@ -14,7 +14,7 @@
 GROUPS = 8
 CLASSES = 4
 SUMMARY, DECAY = range(2)
-PAIR_ADJOINT, PAIR_DECAY, PAIR_PROJ = range(3)
+PAIR_DECAY, PAIR_STEPS, PAIR_PROJ = 0, 1, 6
 PAIR_INPUTS = PAIR_PROJ + 3
 
 
@@ -105,7 +105,13 @@
     pri_re,
     pri_im,
     adj_bf,
-    adj_send,
+    other_adj,
+    other_dec_re,
+    other_dec_im,
+    other_inj_re,
+    other_inj_im,
+    grp_own,
+    grp_other,
     adj_cat,
     z_sum,
     gi_send,
@@ -248,6 +254,13 @@
     dec_im[...] = magnitude * sine
     step_col[...] = wide
 
+    def share(src, dst, at):
+        copy = remote(src, dst, pair_send.at[PAIR_STEPS + at], pair_recv.at[PAIR_STEPS + at], partner)
+        copy.start()
+        return copy
+
+    shared = [share(dec_re, other_dec_re, 0), share(dec_im, other_dec_im, 1)]
+
     def part_dot(whole, weights, owner):
         return dot(whole[owner], weights[pl.ds(pl.multiple_of(owner * width, width), width), :], 1, 0)
 
@@ -275,6 +288,7 @@
     inject += part_dot(cot_all, w_out, across)
     inj_re[...] = inject[:, :states]
     inj_im[...] = -inject[:, states:]
+    shared += [share(inj_re, other_inj_re, 2), share(inj_im, other_inj_im, 3)]
 
     def at_step(j):
         return pl.ds(j, GROUPS, stride=length)
@@ -306,6 +320,8 @@
     for g in range(GROUPS - 2, -1, -1):
         own = compose(own, grp_rows[g])
     z_sum[s] = jnp.concatenate(own, axis=0)
+    for k in range(4):
+        grp_own[k] = grp[k]
 
     def four(ref, at):
         return tuple(ref[at, k : k + 1, :] for k in range(4))
@@ -322,6 +338,7 @@
 
     lax.fori_loop(1, chips, sum_start, 0)
     remote(z_sum.at[s], z_sum.at[s], zs_send.at[SUMMARY], zs_recv.at[SUMMARY], partner).start()
+    shared.append(share(grp_own, grp_other, 4))
     sum_part = z_sum.at[pl.ds(0, seqs - 1)]
     sum_all = remote(sum_part, sum_part, zs_send.at[SUMMARY], zs_recv.at[SUMMARY], partner)
 
@@ -367,14 +384,27 @@
     turned.append(turn(across, 3))
 
     sum_all.wait_recv()
+    end = 2 * z + 1
     in_re, in_im = jnp.zeros((1, states), F32), jnp.zeros((1, states), F32)
-    for j in range(seqs - 1, 0, -1):
+    for j in range(seqs - 1, 1, -1):
         next_re, next_im = pass_on(*four(z_sum, j), in_re, in_im)
-        in_re, in_im = jnp.where(j > s, next_re, in_re), jnp.where(j > s, next_im, in_im)
-    enter = [None] * GROUPS
-    for g in range(GROUPS - 1, -1, -1):
-        enter[g] = (in_re, in_im)
-        in_re, in_im = pass_on(*grp_rows[g], in_re, in_im)
+        in_re, in_im = jnp.where(j > end, next_re, in_re), jnp.where(j > end, next_im, in_im)
+    mid_re, mid_im = pass_on(*four(z_sum, end), in_re, in_im)
+    is_first = c == 0
+
+    def enter(rows, at_re, at_im):
+        found = [None] * GROUPS
+        for g in range(GROUPS - 1, -1, -1):
+            found[g] = (at_re, at_im)
+            at_re, at_im = pass_on(*rows[g], at_re, at_im)
+        return tuple(jnp.concatenate([pair[k] for pair in found], axis=0) for k in range(2))
+
+    for copy in shared:
+        copy.wait_recv()
+    other_rows = [tuple(grp_other[k, g : g + 1, :] for k in range(4)) for g in range(GROUPS)]
+    own_enter = enter(grp_rows, jnp.where(is_first, mid_re, in_re), jnp.where(is_first, mid_im, in_im))
+    other_enter = enter(other_rows, jnp.where(is_first, in_re, mid_re), jnp.where(is_first, in_im, mid_im))
+    first8 = (jnp.zeros((GROUPS, states), jnp.int32) + c) == 0
 
     def back(i, carry):
         at = at_step(length - 1 - i)
@@ -384,28 +414,20 @@
         l_re, l_im = conj_times(dec_re[at, :], dec_im[at, :], a_re, a_im)
         left_re[at, :] = l_re
         left_im[at, :] = l_im
-        return l_re, l_im
-
-    lax.fori_loop(
-        0,
-        length,
-        back,
-        tuple(jnp.concatenate([pair[k] for pair in enter], axis=0) for k in range(2)),
-        unroll=True,
-    )
+        o_re, o_im = other_inj_re[at, :] + carry[2], other_inj_im[at, :] + carry[3]
+        other_adj[at, :] = jnp.where(first8, o_re, o_im)
+        return (l_re, l_im, *conj_times(other_dec_re[at, :], other_dec_im[at, :], o_re, o_im))
+
+    lax.fori_loop(0, length, back, (*own_enter, *other_enter), unroll=True)
     bf_re, bf_im = adj_re[...].astype(BF16), adj_im[...].astype(BF16)
     first = (jnp.zeros((steps, states), jnp.int32) + c) == 0
     own_rows = pl.ds(pl.multiple_of(c * steps, steps), steps)
-    adj_send[...] = jnp.where(first, adj_im[...], adj_re[...]).astype(BF16)
     adj_cat[own_rows, :] = jnp.where(first, adj_re[...], adj_im[...]).astype(BF16)
-    adj_pair = remote(
-        adj_send, adj_cat.at[own_rows], pair_send.at[PAIR_ADJOINT], pair_recv.at[PAIR_ADJOINT], partner
-    )
-    adj_pair.start()
+    other_steps = pl.ds(pl.multiple_of((1 - c) * steps, steps), steps)
+    adj_cat[other_steps, :] = other_adj[...].astype(BF16)
     adj_bf[:, :states] = bf_re
     adj_bf[:, states:] = bf_im
 
-    adj_pair.wait_recv()
     pl.semaphore_wait(known_sem.at[3], batches - 1)
     kind = z % CLASSES
     around = (2, -2, 1, -1, 0)
@@ -584,7 +606,7 @@
 
     for copy in cot_ring + cot_on + inp_ring + inp_on + turned + gi_copies + dec_copies:
         copy.wait_send()
-    for copy in (sum_all, adj_pair, dec_pair, *g_copies.values(), *members, *halves, *wholes, *hands):
+    for copy in (sum_all, dec_pair, *shared, *g_copies.values(), *members, *halves, *wholes, *hands):
         copy.wait_send()
     z_all(z_dec, DECAY).wait_send()
     for copy in (gi_out, gd_out, *gp_outs):
@@ -634,7 +656,9 @@
             pltpu.VMEM((features, 2 * steps), BF16),
             *([per_step] * 13),
             pltpu.VMEM((steps, 2 * states), BF16),
-            pltpu.VMEM((steps, states), BF16),
+            *([per_step] * 5),
+            pltpu.VMEM((4, GROUPS, states), F32),
+            pltpu.VMEM((4, GROUPS, states), F32),
             pltpu.VMEM((2 * steps, states), BF16),
             pltpu.VMEM((seqs, 4, states), F32),
             pltpu.VMEM((blocks - 1, steps, width), BF16),

time: 63.2 us -> 62.9 us (level)
  no operation moved by 1% of the time
where the time goes in v8:
time: 62.9 us; the launch traced here: 62.7 us
  Pallas kernels  62.1 us (99%)
  between operations  0.64 us (1%)
    pallas_call x1, Pallas kernels, local(): pl.pallas_call(functools.partial(kernel, sizes), out_shape=(jax.ShapeDtyp...  60.2 us
    pallas_call x1, Pallas kernels, local(): pl.pallas_call(hand_out, out_shape=[jax.ShapeDtypeStruct(grad_inputs.shap...  1.87 us

profile of v8, /device:TPU:1, one launch (start us, length us, event | category | flops | bytes accessed | tf_op | source)
XLA Modules:
  0.0 62.7 jit_solution(2499026545175823186)
XLA Ops:
  0.6 60.2 %shard_map.112 = (bf16[1,256,512]{2,1,0:T(8,128)(2,1)}, bf16[2,4,128,128]{3,2,1,0:T(8,128)(2,1)}, f32[2,128]{1,0:T(2,128)}) custom-call(bf16[1,256,512]{2,1,0:T(8,128)(2,1)} %cot_ref.1, bf16[1,256,512]{2,1,0:T(8,128)(2,1)} %inp_ref.1, f32[1,256]{1,0:T(1,128)} %step_hbm.1, s32[1,256]{1,0:T(1,128)} %resets_hbm.1, f32[2,128]{1,0:T(2,128)} %rate_hbm.1, ...), custom_call_target="tpu_custom_call" | custom-call | tf_op jit(solution)/shard_map/pallas_call | solution.py:642
  60.8 1.9 %shard_map.113 = (bf16[1,256,512]{2,1,0:T(8,128)(2,1)}, f32[2,512,128]{2,1,0:T(8,128)}, f32[2,128]{1,0:T(2,128)}) custom-call(bf16[1,256,512]{2,1,0:T(8,128)(2,1)} %get-tuple-element.6.gi_in, bf16[2,512,128]{2,1,0:T(8,128)(2,1)} %bitcast.1, f32[2,128]{1,0:T(2,128)} %get-tuple-element.8.gd_in), custom_call_target="tpu_custom_call" | custom-call | tf_op jit(solution)/shard_map/pallas_call | solution.py:706

commit v9 on v8

--- a/solution.py
+++ b/solution.py
@@ -535,7 +535,7 @@
     z_mem[z // CLASSES] = total.astype(BF16)
     member = z_mem.at[z // CLASSES]
     members = []
-    for i in range(chips // CLASSES - 1):
+    for i in sorted(range(chips // CLASSES - 1), key=lambda i: abs(CLASSES * (i + 1) - chips // 2)):
         copy = remote(member, member, zm_send.at[i], zm_recv.at[i], chip(CLASSES * (i + 1)))
         copy.start()
         members.append(copy)

time: 62.9 us -> 62.9 us (level)
  no operation moved by 1% of the time
where the time goes in v9:
time: 62.9 us; the launch traced here: 62.7 us
  Pallas kernels  62.1 us (99%)
  between operations  0.64 us (1%)
    pallas_call x1, Pallas kernels, local(): pl.pallas_call(functools.partial(kernel, sizes), out_shape=(jax.ShapeDtyp...  60.2 us
    pallas_call x1, Pallas kernels, local(): pl.pallas_call(hand_out, out_shape=[jax.ShapeDtypeStruct(grad_inputs.shap...  1.87 us

profile of v9, /device:TPU:1, one launch (start us, length us, event | category | flops | bytes accessed | tf_op | source)
XLA Modules:
  0.0 62.7 jit_solution(2701018842586099847)
XLA Ops:
  0.6 60.2 %shard_map.112 = (bf16[1,256,512]{2,1,0:T(8,128)(2,1)}, bf16[2,4,128,128]{3,2,1,0:T(8,128)(2,1)}, f32[2,128]{1,0:T(2,128)}) custom-call(bf16[1,256,512]{2,1,0:T(8,128)(2,1)} %cot_ref.1, bf16[1,256,512]{2,1,0:T(8,128)(2,1)} %inp_ref.1, f32[1,256]{1,0:T(1,128)} %step_hbm.1, s32[1,256]{1,0:T(1,128)} %resets_hbm.1, f32[2,128]{1,0:T(2,128)} %rate_hbm.1, ...), custom_call_target="tpu_custom_call" | custom-call | tf_op jit(solution)/shard_map/pallas_call | solution.py:642
  60.8 1.9 %shard_map.113 = (bf16[1,256,512]{2,1,0:T(8,128)(2,1)}, f32[2,512,128]{2,1,0:T(8,128)}, f32[2,128]{1,0:T(2,128)}) custom-call(bf16[1,256,512]{2,1,0:T(8,128)(2,1)} %get-tuple-element.6.gi_in, bf16[2,512,128]{2,1,0:T(8,128)(2,1)} %bitcast.1, f32[2,128]{1,0:T(2,128)} %get-tuple-element.8.gd_in), custom_call_target="tpu_custom_call" | custom-call | tf_op jit(solution)/shard_map/pallas_call | solution.py:706
